TPU v7x, 32 devices: a whole 2x2x4 slice. The times are simulated.
32 devices in a mesh: groups: 2 (over y), tile: 16 (over z, x, core).
Axes of the slice: x: 2, y: 2, z: 4, core: 2. Of those that a mesh axis runs over, the one named last changes fastest.
Arguments:
- params: float32 [10, 32, 16, 256], P('groups', 'tile'), parts along dimension 0, may hold values from 0.5 to 4, as said below
- adjoint_state: float32 [16, 2, 9, 8, 16, 256], P('tile', 'groups'), parts along dimension 1, may hold values from -6 to 6
- snapshots: bfloat16 [16, 2, 6, 3, 8, 16, 256], P('tile', 'groups'), parts along dimension 1, may hold values from -6 to 6
- residuals: float32 [16, 2, 6, 256], P('tile', 'groups'), parts along dimension 1, may hold values from -6 to 6
- receivers: int32 [16, 2, 256], P('tile', 'groups'), parts along dimension 1, may hold values from 0 to 32767
- sources: int32 [16, 2], P('tile', 'groups'), parts along dimension 1, may hold values from 0 to 32767
- offsets: int32 [16], P('tile'), may hold values from 0 to 12, as said below
Outputs:
- gradient: float32 [10, 32, 16, 256], P('groups', 'tile'), parts along dimension 0
There are 2 independent parts, one for each index of `groups`. A program takes and returns all parts, laid end to end along the dimension named above; an argument that names none is the same for every part. Nothing has to cross between parts.
Inputs may be any that keep to these rules, and one draw needn't show every extreme that they name: Shot group g's aperture starts at slab offsets[g], with max(0, g - 3) <= offsets[g] <= min(12, g). params holds buoyancy within 0.5 to 1.0, c11 within 2 to 4, c13 within 0.5 to 1.5, c33 within 2 to 4 and c44 within 0.5 to 1.5.
All inputs are finite; a program needn't handle non-finite values. Where the computation divides by a largest or mean magnitude, that divisor is 1e-20 or more.
Results may differ from a plain program's by a relative error of at most 0.0003.
Values sent between devices are 32-bit elements; how exact they have to be, the bound alone decides.
A program may use at most 64 MiB of HBM per device.

v0:
```python
import jax
import jax.numpy as jnp
from jax import lax
from jax.sharding import PartitionSpec as P

STEPS = 6
APER = 4
REACH = 3
MUTE = 4


STEP_H = 0.2
EPSILON = 1e-06


def passed_along(shard, axis, by):
    size = lax.axis_size(axis)
    pairs = [(i, i + by) for i in range(size) if 0 <= i + by < size]
    return lax.ppermute(shard, axis, pairs)


def forward_diff(wavefield, along):
    length = wavefield.shape[along]
    shifted = lax.slice_in_dim(wavefield, 1, length, axis=along)
    border = jnp.zeros_like(lax.slice_in_dim(wavefield, 0, 1, axis=along))
    return jnp.concatenate([shifted, border], axis=along) - wavefield


def backward_diff(wavefield, along):
    length = wavefield.shape[along]
    behind = lax.slice_in_dim(wavefield, 0, length - 1, axis=along)
    border = jnp.zeros_like(lax.slice_in_dim(wavefield, 0, 1, axis=along))
    return wavefield - jnp.concatenate([border, behind], axis=along)


def strains(velocity_x, velocity_y, velocity_z):
    strain_xx = backward_diff(velocity_x, 0)
    strain_yy = backward_diff(velocity_y, 1)
    strain_zz = backward_diff(velocity_z, 2)
    strain_xy = forward_diff(velocity_x, 1) + forward_diff(velocity_y, 0)
    strain_xz = forward_diff(velocity_x, 2) + forward_diff(velocity_z, 0)
    strain_yz = forward_diff(velocity_y, 2) + forward_diff(velocity_z, 1)
    return (strain_xx, strain_yy, strain_zz, strain_xy, strain_xz, strain_yz)


def mute_weight(source, grid_shape):
    plane_cells = grid_shape[1] * grid_shape[2]
    source_x = (source // plane_cells).astype(jnp.float32)
    source_y = (source // grid_shape[2] % grid_shape[1]).astype(jnp.float32)
    source_z = (source % grid_shape[2]).astype(jnp.float32)
    delta_x = lax.broadcasted_iota(jnp.float32, grid_shape, 0) - source_x
    delta_y = lax.broadcasted_iota(jnp.float32, grid_shape, 1) - source_y
    delta_z = lax.broadcasted_iota(jnp.float32, grid_shape, 2) - source_z
    distance = delta_x * delta_x + delta_y * delta_y + delta_z * delta_z
    return distance / (distance + float(MUTE * MUTE))


def shot_gradient(aperture, adjoint, snapshot, residual, receiver, source):
    buoyancy, stiff_11, stiff_13, stiff_33, stiff_44 = (
        aperture[0],
        aperture[1],
        aperture[2],
        aperture[3],
        aperture[4],
    )
    stiff_66 = 0.5 * (stiff_11 - stiff_13)
    velocity_x, velocity_y, velocity_z = (adjoint[0], adjoint[1], adjoint[2])
    stress_xx, stress_yy, stress_zz = (adjoint[3], adjoint[4], adjoint[5])
    stress_xy, stress_xz, stress_yz = (adjoint[6], adjoint[7], adjoint[8])
    grid_shape = velocity_x.shape
    kernel_b = jnp.zeros(grid_shape, jnp.float32)
    kernel_11 = jnp.zeros(grid_shape, jnp.float32)
    kernel_13 = jnp.zeros(grid_shape, jnp.float32)
    kernel_33 = jnp.zeros(grid_shape, jnp.float32)
    kernel_44 = jnp.zeros(grid_shape, jnp.float32)
    for step_index in range(STEPS):
        velocity_x = velocity_x + STEP_H * buoyancy * (
            forward_diff(stress_xx, 0) + backward_diff(stress_xy, 1) + backward_diff(stress_xz, 2)
        )
        velocity_y = velocity_y + STEP_H * buoyancy * (
            backward_diff(stress_xy, 0) + forward_diff(stress_yy, 1) + backward_diff(stress_yz, 2)
        )
        velocity_z = velocity_z + STEP_H * buoyancy * (
            backward_diff(stress_xz, 0) + backward_diff(stress_yz, 1) + forward_diff(stress_zz, 2)
        )
        velocity_z = (
            velocity_z.reshape(-1).at[receiver].add(residual[step_index]).reshape(grid_shape)
        )
        strain_xx, strain_yy, strain_zz, strain_xy, strain_xz, strain_yz = strains(
            velocity_x, velocity_y, velocity_z
        )
        stress_xx = stress_xx + STEP_H * (stiff_11 * strain_xx + stiff_13 * (strain_yy + strain_zz))
        stress_yy = stress_yy + STEP_H * (stiff_11 * strain_yy + stiff_13 * (strain_xx + strain_zz))
        stress_zz = stress_zz + STEP_H * (stiff_13 * (strain_xx + strain_yy) + stiff_33 * strain_zz)
        stress_xy = stress_xy + STEP_H * stiff_66 * strain_xy
        stress_xz = stress_xz + STEP_H * stiff_44 * strain_xz
        stress_yz = stress_yz + STEP_H * stiff_44 * strain_yz
        forward_x = snapshot[step_index, 0].astype(jnp.float32)
        forward_y = snapshot[step_index, 1].astype(jnp.float32)
        forward_z = snapshot[step_index, 2].astype(jnp.float32)
        forward_xx, forward_yy, forward_zz, forward_xy, forward_xz, forward_yz = strains(
            forward_x, forward_y, forward_z
        )
        kernel_b = (
            kernel_b + velocity_x * forward_x + velocity_y * forward_y + velocity_z * forward_z
        )
        kernel_11 = (
            kernel_11
            + strain_xx * forward_xx
            + strain_yy * forward_yy
            + 0.5 * strain_xy * forward_xy
        )
        kernel_13 = (
            kernel_13
            + strain_xx * (forward_yy + forward_zz)
            + strain_yy * (forward_xx + forward_zz)
            + strain_zz * (forward_xx + forward_yy)
            - 0.5 * strain_xy * forward_xy
        )
        kernel_33 = kernel_33 + strain_zz * forward_zz
        kernel_44 = kernel_44 + strain_xz * forward_xz + strain_yz * forward_yz
    weight = mute_weight(source, grid_shape)
    return jnp.stack([kernel_b, kernel_11, kernel_13, kernel_33, kernel_44]) * weight


def on_device(params, adjoint_state, snapshots, residuals, receivers, sources, offsets):
    tile_index = lax.axis_index("tile")
    slab_cells = params.shape[1]
    span_count = 2 * REACH + 1
    cross_shape = params.shape[2:]
    field_count = params.shape[0]
    pieces = []
    for position in range(span_count):
        if position == REACH:
            pieces.append(params)
        else:
            pieces.append(passed_along(params, "tile", REACH - position))
    window = jnp.concatenate(pieces, axis=1)
    relative = offsets[0] - tile_index + REACH
    aperture = lax.dynamic_slice_in_dim(window, relative * slab_cells, APER * slab_cells, axis=1)
    contrib = shot_gradient(
        aperture,
        adjoint_state[0, 0],
        snapshots[0, 0],
        residuals[0, 0],
        receivers[0, 0],
        sources[0, 0],
    )
    empty_window = jnp.zeros((field_count, span_count * slab_cells) + cross_shape, jnp.float32)
    grad_window = lax.dynamic_update_slice_in_dim(
        empty_window, contrib, relative * slab_cells, axis=1
    )
    own_part = grad_window[:, REACH * slab_cells : (REACH + 1) * slab_cells]
    summed = own_part
    for position in range(span_count):
        if position != REACH:
            outgoing = grad_window[:, position * slab_cells : (position + 1) * slab_cells]
            summed = summed + passed_along(outgoing, "tile", position - REACH)
    largest = jnp.max(jnp.abs(summed), axis=(1, 2, 3))
    largest = lax.pmax(largest, "tile")
    return summed / (largest[:, None, None, None] + EPSILON)


def solution(mesh):
    placed = (
        P("groups", "tile", None, None),
        P("tile", "groups", None, None, None, None),
        P("tile", "groups", None, None, None, None, None),
        P("tile", "groups", None, None),
        P("tile", "groups", None),
        P("tile", "groups"),
        P("tile"),
    )
    return jax.shard_map(
        on_device,
        mesh=mesh,
        in_specs=placed,
        out_specs=P("groups", "tile", None, None),
        check_vma=False,
    )
```

profile of v0, /device:TPU:0, one launch (start us, length us, event | category | flops | bytes accessed | tf_op | source)
XLA Modules:
  0.0 206.5 jit_solution(3448066671280516047)
XLA Ops:
  0.0 5.1 %collective-permute-start = (f32[5,2,16,256]{3,2,1,0:T(8,128)}, f32[5,2,16,256]{3,2,1,0:T(8,128)}, u32[]{:S(2)}, u32[]{:S(2)}) collective-permute-start(f32[5,2,16,256]{3,2,1,0:T(8,128)} %param.7), channel_id=1, source_target_pairs={{0,3},{1,4},{2,5},{3,6},{4,7},{5,8},{6,9},{7,10},{8,11},{9,12},{10... | collective-permute-start | bytes 491528 | tf_op jit(solution)/shard_map/ppermute | solution.py:19
  5.1 4.1 %collective-permute-start.1 = (f32[5,2,16,256]{3,2,1,0:T(8,128)}, f32[5,2,16,256]{3,2,1,0:T(8,128)}, u32[]{:S(2)}, u32[]{:S(2)}) collective-permute-start(f32[5,2,16,256]{3,2,1,0:T(8,128)} %param.7), channel_id=1, source_target_pairs={{0,2},{1,3},{2,4},{3,5},{4,6},{5,7},{6,8},{7,9},{8,10},{9,11},{10,... | collective-permute-start | bytes 491528 | tf_op jit(solution)/shard_map/ppermute | solution.py:19
  9.2 2.3 %collective-permute-start.2 = (f32[5,2,16,256]{3,2,1,0:T(8,128)}, f32[5,2,16,256]{3,2,1,0:T(8,128)}, u32[]{:S(2)}, u32[]{:S(2)}) collective-permute-start(f32[5,2,16,256]{3,2,1,0:T(8,128)} %param.7), channel_id=1, source_target_pairs={{0,1},{1,2},{2,3},{3,4},{4,5},{5,6},{6,7},{7,8},{8,9},{9,10},{10,1... | collective-permute-start | bytes 491528 | tf_op jit(solution)/shard_map/ppermute | solution.py:19
  14.1 2.0 slice_bitcast_fusion.4
  59.2 2.0 collective-permute-done.5
  63.1 2.0 scatter_fusion
  67.3 2.2 %multiply_add_fusion.43 = (f32[8,16,256]{2,1,0:T(8,128)S(1)}, f32[8,16,256]{2,1,0:T(8,128)}, f32[8,16,256]{2,1,0:T(8,128)S(1)}, f32[8,16,256]{2,1,0:T(8,128)S(1)...) fusion(f32[1,1,9,8,16,256]{5,4,3,2,1,0:T(8,128)} %param.8, ...), kind=kLoop, calls=%fused_computation.131 | loop fusion | flops 720896 | bytes 3218448 | tf_op jit(solution)/shard_map/add | solution.py:95
  69.5 2.1 %bitcast_add_fusion.2 = (f32[8,16,256]{2,1,0:T(8,128)S(1)}, f32[8,16,256]{2,1,0:T(8,128)S(1)}, f32[8,16,256]{2,1,0:T(8,128)S(1)}, f32[8,16,256]{2,1,0:T(8,128)}) fusion(f32[8,16,256]{2,1,0:T(8,128)S(1)} %get-tuple-element.72, f32[8,16,256]{2,1,0:T(8,128)S(1)} %get-tuple-element.70, f32[8,16,256]{2,1,0:T(8,128)S(1)} %get-tuple-element.71, ...), kind=kLoop, calls=%fused_computation.29 | loop fusion | flops 589824 | bytes 2342420 | tf_op jit(solution)/shard_map/add | solution.py:92
  73.4 2.0 scatter_fusion.1
  79.0 2.2 %multiply_add_fusion.33 = (f32[8,16,256]{2,1,0:T(8,128)S(1)}, f32[8,16,256]{2,1,0:T(8,128)}, f32[8,16,256]{2,1,0:T(8,128)S(1)}, f32[8,16,256]{2,1,0:T(8,128)S(1)...) fusion(f32[8,16,256]{2,1,0:T(8,128)S(1)} %get-tuple-element.75,, ...), kind=kLoop, calls=%fused_computation.114 | loop fusion | flops 655360 | bytes 3095056 | tf_op jit(solution)/shard_map/add | solution.py:96
  86.8 2.0 scatter_fusion.2
  94.3 2.2 %multiply_add_fusion.24 = (f32[8,16,256]{2,1,0:T(8,128)S(1)}, f32[8,16,256]{2,1,0:T(8,128)}, f32[8,16,256]{2,1,0:T(8,128)S(1)}, f32[8,16,256]{2,1,0:T(8,128)S(1)...) fusion(f32[8,16,256]{2,1,0:T(8,128)S(1)} %copy-done.20, ...), kind=kLoop, calls=%fused_computation.99 | loop fusion | flops 655360 | bytes 3095056 | tf_op jit(solution)/shard_map/add | solution.py:96
  101.9 2.2 %scatter_fusion.3 = f32[32768]{0:T(1024)S(1)} fusion(f32[32768]{0:T(1024)S(1)} %bitcast.549, s32[256]{0:T(256)S(1)} %bitcast.622, f32[256]{0:T(256)S(1)} %bitcast.627), kind=kCustom, calls=%fused_computation.3 | custom fusion | flops 256 | bytes 4096 | tf_op jit(solution)/shard_map/scatter-add | solution.py:87
  110.2 2.2 %multiply_add_fusion.15 = (f32[8,16,256]{2,1,0:T(8,128)S(1)}, f32[8,16,256]{2,1,0:T(8,128)}, f32[8,16,256]{2,1,0:T(8,128)S(1)}, f32[8,16,256]{2,1,0:T(8,128)S(1)...) fusion(f32[8,16,256]{2,1,0:T(8,128)} %copy-done.21, ...), kind=kLoop, calls=%fused_computation.84 | loop fusion | flops 655360 | bytes 3095056 | tf_op jit(solution)/shard_map/add | solution.py:96
  117.8 2.0 scatter_fusion.4
  126.6 2.3 %multiply_add_fusion.6 = (f32[8,16,256]{2,1,0:T(8,128)S(1)}, f32[8,16,256]{2,1,0:T(8,128)}, f32[8,16,256]{2,1,0:T(8,128)}, f32[8,16,256]{2,1,0:T(8,128)S(1)}, f3...) fusion(f32[8,16,256]{2,1,0:T(8,128)} %copy-done.18, ...), kind=kLoop, calls=%fused_computation.69 | loop fusion | flops 655360 | bytes 3095056 | tf_op jit(solution)/shard_map/add | solution.py:96
  129.9 2.0 scatter_fusion.5
  133.0 3.1 %bitcast_dynamic-update-slice_fusion.4 = (f32[5,8,16,256]{3,2,1,0:T(8,128)}, f32[8,16,256]{2,1,0:T(8,128)S(1)}, f32[8,16,256]{2,1,0:T(8,128)S(1)}) fusion(f32[8,16,256]{2,1,0:T(8,128)S(1)} %reshape.208, f32[8,16,256]{2,1,0:T(8,128)} %reshape.206, f32[8,16,256]{2,1,0:T(8,128)} %copy-done.8, f32[8,16,256]{2,1,0:T(8,128)} %copy-done.7, ...), kind=kLoop, calls=%fused_computation.26 | loop fusion | flops 2228223 | bytes 5192708
  139.4 3.0 %bitcast_dynamic-update-slice_fusion.3 = (f32[5,8,16,256]{3,2,1,0:T(8,128)}, f32[8,16,256]{2,1,0:T(8,128)S(1)}, f32[8,16,256]{2,1,0:T(8,128)S(1)}, f32[8,16,256]...) fusion(f32[5,8,16,256]{3,2,1,0:T(8,128)} %get-tuple-element.13, ...), kind=kLoop, calls=%fused_computation.25 | loop fusion | flops 2883584 | bytes 7143424
  146.1 3.8 %bitcast_dynamic-update-slice_fusion = f32[5,8,16,256]{3,2,1,0:T(8,128)} fusion(f32[5,8,16,256]{3,2,1,0:T(8,128)} %bitcast_dynamic-update-slice_fusion.1, f32[8,15,256]{2,1,0:T(8,128)} %slice.1178, f32[8,16,255]{2,1,0:T(8,128)} %slice.1177, f32[8,16,256]{2,1,0:T(8,128)S(1)} %reshape.208, f32[8,15,256]{2,1,0:T(8,128)} %slice.1176, ...), kind=kLoop, calls=%fused_computation.22 | loop fusion | flops 2719744 | bytes 6569472 | tf_op jit(solution)/shard_map/stack | solution.py:123
  152.0 5.5 %collective-permute-start.10 = (f32[5,2,16,256]{3,2,1,0:T(8,128)S(1)}, f32[5,2,16,256]{3,2,1,0:T(8,128)S(1)}, u32[]{:S(2)}, u32[]{:S(2)}) collective-permute-start(f32[5,2,16,256]{3,2,1,0:T(8,128)S(1)} %get-tuple-element.165), channel_id=1, source_target_pairs={{0,2},{1,3},{2,4},{3,5},{4,6},{5,7},{6,8},{7,9},{8,10},{9,11},{10,... | collective-permute-start | bytes 491528 | tf_op jit(solution)/shard_map/ppermute | solution.py:19
  157.5 2.9 %collective-permute-start.11 = (f32[5,2,16,256]{3,2,1,0:T(8,128)S(1)}, f32[5,2,16,256]{3,2,1,0:T(8,128)S(1)}, u32[]{:S(2)}, u32[]{:S(2)}) collective-permute-start(f32[5,2,16,256]{3,2,1,0:T(8,128)S(1)} %get-tuple-element.164), channel_id=1, source_target_pairs={{0,3},{1,4},{2,5},{3,6},{4,7},{5,8},{6,9},{7,10},{8,11},{9,12},{10... | collective-permute-start | bytes 491528 | tf_op jit(solution)/shard_map/ppermute | solution.py:19
  164.3 4.3 %collective-permute-start.9 = (f32[5,2,16,256]{3,2,1,0:T(8,128)S(1)}, f32[5,2,16,256]{3,2,1,0:T(8,128)S(1)}, u32[]{:S(2)}, u32[]{:S(2)}) collective-permute-start(f32[5,2,16,256]{3,2,1,0:T(8,128)S(1)} %get-tuple-element.166), channel_id=1, source_target_pairs={{0,1},{1,2},{2,3},{3,4},{4,5},{5,6},{6,7},{7,8},{8,9},{9,10},{10,1... | collective-permute-start | bytes 491528 | tf_op jit(solution)/shard_map/ppermute | solution.py:19
  170.0 35.8 %pmax.7 = f32[5]{0:T(128)S(1)} all-reduce(f32[5]{0:T(128)S(1)} %get-tuple-element.5), channel_id=1, replica_groups=mesh['groups'=2,'tile'=16] {'tile'}, use_global_device_ids=true, to_apply=%region_7.8 | all-reduce | flops 5 | bytes 40 | tf_op jit(solution)/shard_map/pmax | solution.py:160
  (486 shorter events, 103.6 us)
Async XLA Ops:
  0.0 53.0 %collective-permute-start = (f32[5,2,16,256]{3,2,1,0:T(8,128)}, f32[5,2,16,256]{3,2,1,0:T(8,128)}, u32[]{:S(2)}, u32[]{:S(2)}) collective-permute-start(f32[5,2,16,256]{3,2,1,0:T(8,128)} %param.7), channel_id=1, source_target_pairs={{0,3},{1,4},{2,5},{3,6},{4,7},{5,8},{6,9},{7,10},{8,11},{9,12},{10... | collective-permute-start | bytes 491528 | tf_op jit(solution)/shard_map/ppermute | solution.py:19
  5.1 50.3 %collective-permute-start.1 = (f32[5,2,16,256]{3,2,1,0:T(8,128)}, f32[5,2,16,256]{3,2,1,0:T(8,128)}, u32[]{:S(2)}, u32[]{:S(2)}) collective-permute-start(f32[5,2,16,256]{3,2,1,0:T(8,128)} %param.7), channel_id=1, source_target_pairs={{0,2},{1,3},{2,4},{3,5},{4,6},{5,7},{6,8},{7,9},{8,10},{9,11},{10,... | collective-permute-start | bytes 491528 | tf_op jit(solution)/shard_map/ppermute | solution.py:19
  9.2 47.1 %collective-permute-start.2 = (f32[5,2,16,256]{3,2,1,0:T(8,128)}, f32[5,2,16,256]{3,2,1,0:T(8,128)}, u32[]{:S(2)}, u32[]{:S(2)}) collective-permute-start(f32[5,2,16,256]{3,2,1,0:T(8,128)} %param.7), channel_id=1, source_target_pairs={{0,1},{1,2},{2,3},{3,4},{4,5},{5,6},{6,7},{7,8},{8,9},{9,10},{10,1... | collective-permute-start | bytes 491528 | tf_op jit(solution)/shard_map/ppermute | solution.py:19
  11.5 45.7 %collective-permute-start.3 = (f32[5,2,16,256]{3,2,1,0:T(8,128)}, f32[5,2,16,256]{3,2,1,0:T(8,128)}, u32[]{:S(2)}, u32[]{:S(2)}) collective-permute-start(f32[5,2,16,256]{3,2,1,0:T(8,128)} %param.7), channel_id=1, source_target_pairs={{1,0},{2,1},{3,2},{4,3},{5,4},{6,5},{7,6},{8,7},{9,8},{10,9},{11,1... | collective-permute-start | bytes 491528 | tf_op jit(solution)/shard_map/ppermute | solution.py:19
  12.8 45.4 %collective-permute-start.4 = (f32[5,2,16,256]{3,2,1,0:T(8,128)}, f32[5,2,16,256]{3,2,1,0:T(8,128)}, u32[]{:S(2)}, u32[]{:S(2)}) collective-permute-start(f32[5,2,16,256]{3,2,1,0:T(8,128)} %param.7), channel_id=1, source_target_pairs={{2,0},{3,1},{4,2},{5,3},{6,4},{7,5},{8,6},{9,7},{10,8},{11,9},{12,... | collective-permute-start | bytes 491528 | tf_op jit(solution)/shard_map/ppermute | solution.py:19
  20.3 24.0 %copy-start.42 = (f32[8,16,256]{2,1,0:T(8,128)}, f32[8,16,256]{2,1,0:T(8,128)S(1)}, u32[]{:S(2)}) copy-start(f32[8,16,256]{2,1,0:T(8,128)S(1)} %get-tuple-element.135) | copy-start | bytes 393220
  20.3 24.8 %copy-start.74 = (f32[8,16,256]{2,1,0:T(8,128)}, f32[8,16,256]{2,1,0:T(8,128)S(1)}, u32[]{:S(2)}) copy-start(f32[8,16,256]{2,1,0:T(8,128)S(1)} %get-tuple-element.134) | copy-start | bytes 393220
  20.3 25.5 %copy-start.40 = (f32[8,16,256]{2,1,0:T(8,128)}, f32[8,16,256]{2,1,0:T(8,128)S(1)}, u32[]{:S(2)}) copy-start(f32[8,16,256]{2,1,0:T(8,128)S(1)} %get-tuple-element.131) | copy-start | bytes 393220
  20.3 26.2 %copy-start.70 = (f32[8,16,256]{2,1,0:T(8,128)}, f32[8,16,256]{2,1,0:T(8,128)S(1)}, u32[]{:S(2)}) copy-start(f32[8,16,256]{2,1,0:T(8,128)S(1)} %get-tuple-element.130) | copy-start | bytes 393220
  20.3 26.9 %copy-start.38 = (f32[8,16,256]{2,1,0:T(8,128)}, f32[8,16,256]{2,1,0:T(8,128)S(1)}, u32[]{:S(2)}) copy-start(f32[8,16,256]{2,1,0:T(8,128)S(1)} %get-tuple-element.127) | copy-start | bytes 393220
  20.3 27.6 %copy-start.68 = (f32[8,16,256]{2,1,0:T(8,128)}, f32[8,16,256]{2,1,0:T(8,128)S(1)}, u32[]{:S(2)}) copy-start(f32[8,16,256]{2,1,0:T(8,128)S(1)} %get-tuple-element.126) | copy-start | bytes 393220
  20.4 28.3 %copy-start.36 = (f32[8,16,256]{2,1,0:T(8,128)}, f32[8,16,256]{2,1,0:T(8,128)S(1)}, u32[]{:S(2)}) copy-start(f32[8,16,256]{2,1,0:T(8,128)S(1)} %get-tuple-element.123) | copy-start | bytes 393220
  20.4 29.1 %copy-start.64 = (f32[8,16,256]{2,1,0:T(8,128)}, f32[8,16,256]{2,1,0:T(8,128)S(1)}, u32[]{:S(2)}) copy-start(f32[8,16,256]{2,1,0:T(8,128)S(1)} %get-tuple-element.122) | copy-start | bytes 393220
  20.4 29.7 %copy-start.34 = (f32[8,16,256]{2,1,0:T(8,128)}, f32[8,16,256]{2,1,0:T(8,128)S(1)}, u32[]{:S(2)}) copy-start(f32[8,16,256]{2,1,0:T(8,128)S(1)} %get-tuple-element.120) | copy-start | bytes 393220
  20.4 30.5 %copy-start.66 = (f32[8,16,256]{2,1,0:T(8,128)}, f32[8,16,256]{2,1,0:T(8,128)S(1)}, u32[]{:S(2)}) copy-start(f32[8,16,256]{2,1,0:T(8,128)S(1)} %get-tuple-element.124) | copy-start | bytes 393220
  20.4 31.1 %copy-start.44 = (f32[8,16,256]{2,1,0:T(8,128)}, f32[8,16,256]{2,1,0:T(8,128)S(1)}, u32[]{:S(2)}) copy-start(f32[8,16,256]{2,1,0:T(8,128)S(1)} %get-tuple-element.136) | copy-start | bytes 393220
  20.4 31.9 %copy-start.72 = (f32[8,16,256]{2,1,0:T(8,128)}, f32[8,16,256]{2,1,0:T(8,128)S(1)}, u32[]{:S(2)}) copy-start(f32[8,16,256]{2,1,0:T(8,128)S(1)} %get-tuple-element.132) | copy-start | bytes 393220
  53.0 8.1 %collective-permute-start.5 = (f32[5,2,16,256]{3,2,1,0:T(8,128)S(1)}, f32[5,2,16,256]{3,2,1,0:T(8,128)S(1)}, u32[]{:S(2)}, u32[]{:S(2)}) collective-permute-start(f32[5,2,16,256]{3,2,1,0:T(8,128)S(1)} %copy-done.145), channel_id=1, source_target_pairs={{3,0},{4,1},{5,2},{6,3},{7,4},{8,5},{9,6},{10,7},{11,8},{12,9},{13... | collective-permute-start | bytes 491528 | tf_op jit(solution)/shard_map/ppermute | solution.py:19
  152.0 12.3 %collective-permute-start.10 = (f32[5,2,16,256]{3,2,1,0:T(8,128)S(1)}, f32[5,2,16,256]{3,2,1,0:T(8,128)S(1)}, u32[]{:S(2)}, u32[]{:S(2)}) collective-permute-start(f32[5,2,16,256]{3,2,1,0:T(8,128)S(1)} %get-tuple-element.165), channel_id=1, source_target_pairs={{0,2},{1,3},{2,4},{3,5},{4,6},{5,7},{6,8},{7,9},{8,10},{9,11},{10,... | collective-permute-start | bytes 491528 | tf_op jit(solution)/shard_map/ppermute | solution.py:19
  157.5 11.2 %collective-permute-start.11 = (f32[5,2,16,256]{3,2,1,0:T(8,128)S(1)}, f32[5,2,16,256]{3,2,1,0:T(8,128)S(1)}, u32[]{:S(2)}, u32[]{:S(2)}) collective-permute-start(f32[5,2,16,256]{3,2,1,0:T(8,128)S(1)} %get-tuple-element.164), channel_id=1, source_target_pairs={{0,3},{1,4},{2,5},{3,6},{4,7},{5,8},{6,9},{7,10},{8,11},{9,12},{10... | collective-permute-start | bytes 491528 | tf_op jit(solution)/shard_map/ppermute | solution.py:19
  160.4 8.3 %collective-permute-start.6 = (f32[5,2,16,256]{3,2,1,0:T(8,128)S(1)}, f32[5,2,16,256]{3,2,1,0:T(8,128)S(1)}, u32[]{:S(2)}, u32[]{:S(2)}) collective-permute-start(f32[5,2,16,256]{3,2,1,0:T(8,128)S(1)} %get-tuple-element.163), channel_id=1, source_target_pairs={{3,0},{4,1},{5,2},{6,3},{7,4},{8,5},{9,6},{10,7},{11,8},{12,9},{13... | collective-permute-start | bytes 491528 | tf_op jit(solution)/shard_map/ppermute | solution.py:19
  161.7 8.2 %collective-permute-start.7 = (f32[5,2,16,256]{3,2,1,0:T(8,128)S(1)}, f32[5,2,16,256]{3,2,1,0:T(8,128)S(1)}, u32[]{:S(2)}, u32[]{:S(2)}) collective-permute-start(f32[5,2,16,256]{3,2,1,0:T(8,128)S(1)} %get-tuple-element.168), channel_id=1, source_target_pairs={{2,0},{3,1},{4,2},{5,3},{6,4},{7,5},{8,6},{9,7},{10,8},{11,9},{12,... | collective-permute-start | bytes 491528 | tf_op jit(solution)/shard_map/ppermute | solution.py:19
  163.0 6.9 %collective-permute-start.8 = (f32[5,2,16,256]{3,2,1,0:T(8,128)S(1)}, f32[5,2,16,256]{3,2,1,0:T(8,128)S(1)}, u32[]{:S(2)}, u32[]{:S(2)}) collective-permute-start(f32[5,2,16,256]{3,2,1,0:T(8,128)S(1)} %get-tuple-element.167), channel_id=1, source_target_pairs={{1,0},{2,1},{3,2},{4,3},{5,4},{6,5},{7,6},{8,7},{9,8},{10,9},{11,1... | collective-permute-start | bytes 491528 | tf_op jit(solution)/shard_map/ppermute | solution.py:19
  164.3 5.6 %collective-permute-start.9 = (f32[5,2,16,256]{3,2,1,0:T(8,128)S(1)}, f32[5,2,16,256]{3,2,1,0:T(8,128)S(1)}, u32[]{:S(2)}, u32[]{:S(2)}) collective-permute-start(f32[5,2,16,256]{3,2,1,0:T(8,128)S(1)} %get-tuple-element.166), channel_id=1, source_target_pairs={{0,1},{1,2},{2,3},{3,4},{4,5},{5,6},{6,7},{7,8},{8,9},{9,10},{10,1... | collective-permute-start | bytes 491528 | tf_op jit(solution)/shard_map/ppermute | solution.py:19
  (141 other events, 586.8 us)
where the time goes:
time: 208 us; the launch traced here: 207 us
  local copies, waits for them, and re-layouts  79 us (38%)
  other arithmetic  52.8 us (25%)
  blocking collectives  35.8 us (17%)
  starting transfers between devices  32.1 us (15%)
  between operations  3.65 us (2%)
  waiting for transfers between devices  3.19 us (2%)
    slice x88, local copies, waits for them, and re-layouts, forward_diff(): shifted = lax.slice_in_dim(wavefield, 1, length, axis=along)  51.8 us
    pmax x1, blocking collectives, on_device(): largest = lax.pmax(largest, 'tile')  35.8 us
    ppermute x12, starting transfers between devices, passed_along(): return lax.ppermute(shard, axis, pairs)  32.1 us
    slice x22, local copies, waits for them, and re-layouts, backward_diff(): behind = lax.slice_in_dim(wavefield, 0, length - 1, axis=along)  12.4 us
    scatter-add x6, other arithmetic, shot_gradient(): velocity_z.reshape(-1).at[receiver].add(residual[step_index])  12.3 us
    unnamed x318, local copies, waits for them, and re-layouts  11 us
    add x4, other arithmetic, shot_gradient(): stress_xz = stress_xz + STEP_H * stiff_44 * strain_xz  8.86 us
    unnamed x4, other arithmetic  8.63 us
  transfers between devices with their start and end apart: 12, of which 2 were waited for; matrix products, arithmetic and copies ran while one was open for 20% of the time, Pallas kernels for 0%

commit v1 on v0

v1 whole, which is shorter than its diff:
```python
import functools

import jax
import jax.numpy as jnp
from jax import lax
from jax.experimental import pallas as pl
from jax.experimental.pallas import tpu as pltpu
from jax.sharding import PartitionSpec as P

STEPS = 6
APER = 4
REACH = 3
MUTE = 4
SPAN = 2 * REACH + 1

STEP_H = 0.2
EPSILON = 1e-06
MESH = pl.DeviceIdType.MESH


def shift_up(plane, axis):
    size = plane.shape[axis]
    place = lax.broadcasted_iota(jnp.int32, plane.shape, axis)
    return jnp.where(place == size - 1, 0.0, pltpu.roll(plane, size - 1, axis))


def shift_down(plane, axis):
    place = lax.broadcasted_iota(jnp.int32, plane.shape, axis)
    return jnp.where(place == 0, 0.0, pltpu.roll(plane, 1, axis))


def fwd(plane, axis):
    return shift_up(plane, axis) - plane


def bwd(plane, axis):
    return plane - shift_down(plane, axis)


def strains_at(here, before, after):
    vx, vy, vz = here
    exx = vx if before is None else vx - before
    eyy = bwd(vy, 0)
    ezz = bwd(vz, 1)
    if after is None:
        exy = fwd(vx, 0) - vy
        exz = fwd(vx, 1) - vz
    else:
        exy = fwd(vx, 0) + (after[0] - vy)
        exz = fwd(vx, 1) + (after[1] - vz)
    eyz = fwd(vy, 1) + fwd(vz, 0)
    return exx, eyy, ezz, exy, exz, eyz


def kernel(
    tiles,
    offsets,
    sources,
    params,
    adjoint,
    snapshots,
    residuals,
    receivers,
    out,
    window,
    state,
    snaps,
    inject,
    fstrain,
    coef,
    grad,
    gwin,
    fromp,
    sumbuf,
    landed,
    mine,
    maxima,
    local_sem,
    p_send,
    p_recv,
    g_send,
    g_recv,
    m_send,
    m_recv,
):
    me = lax.axis_index("tile")
    core = lax.rem(me, 2)
    partner = me + 1 - 2 * core
    far = me + 3 * (2 * core - 1)
    nx = state.shape[1]
    slab = params.shape[1]
    ny, nz = state.shape[2], state.shape[3]

    own_copy = pltpu.make_async_copy(params, window.at[REACH], local_sem.at[0])
    state_copy = pltpu.make_async_copy(adjoint.at[0, 0], state, local_sem.at[1])
    snap_copy = pltpu.make_async_copy(snapshots.at[0, 0], snaps, local_sem.at[2])
    own_copy.start()
    snap_copy.start()
    state_copy.start()

    barrier = pltpu.get_barrier_semaphore()

    @pl.loop(1, tiles)
    def _(d):
        pl.semaphore_signal(
            barrier, inc=1, device_id={"tile": lax.rem(me + d, tiles)}, device_id_type=MESH
        )

    pl.semaphore_wait(barrier, tiles - 1)

    def inside(t):
        return jnp.logical_and(t >= 0, t < tiles)

    def push(src, dst, sems, recvs, s, r, to):
        return pltpu.make_async_remote_copy(
            src_ref=src,
            dst_ref=dst,
            send_sem=sems.at[s],
            recv_sem=recvs.at[r],
            device_id={"tile": to},
            device_id_type=MESH,
        )

    def when_in(t, fn):
        pl.when(inside(t))(fn)

    send_far = push(params, window.at[6 * (1 - core)], p_send, p_recv, 0, 6 * (1 - core), far)
    send_up = push(params, window.at[1], p_send, p_recv, 1, 1, me + 2)
    send_dn = push(params, window.at[5], p_send, p_recv, 2, 5, me - 2)
    send_pa = push(params, window.at[2 + 2 * core], p_send, p_recv, 3, 2 + 2 * core, partner)
    when_in(me + 2, send_up.start)
    when_in(me - 2, send_dn.start)
    when_in(far, send_far.start)
    send_pa.start()

    cells = receivers[...]
    lanes = cells.shape[1]
    rows = nx * ny
    row_of = lax.div(cells, nz)
    col_of = lax.rem(cells, nz)
    row_hit = lax.broadcasted_iota(jnp.int32, (rows, lanes), 0) == row_of
    col_hit = lax.broadcasted_iota(jnp.int32, (nz, lanes), 0) == col_of
    columns = jnp.where(col_hit, 1.0, 0.0).astype(jnp.bfloat16)
    for s in range(STEPS):
        rest = residuals[0, 0, s : s + 1, :]
        total = None
        for part in range(3):
            piece = rest.astype(jnp.bfloat16).astype(jnp.float32)
            rest = rest - piece
            left = jnp.where(row_hit, piece, 0.0).astype(jnp.bfloat16)
            term = lax.dot_general(
                left, columns, (((1,), (1,)), ((), ())), preferred_element_type=jnp.float32
            )
            total = term if total is None else total + term
        inject[s] = total.reshape(nx, ny, nz)

    snap_copy.wait()

    @pl.loop(0, STEPS)
    def _(s):
        u = [[snaps[s, c, i].astype(jnp.float32) for i in range(nx)] for c in range(3)]
        for i in range(nx):
            here = (u[0][i], u[1][i], u[2][i])
            before = u[0][i - 1] if i > 0 else None
            after = (u[1][i + 1], u[2][i + 1]) if i + 1 < nx else None
            f = strains_at(here, before, after)
            for k in range(6):
                fstrain[s, k, i] = 0.5 * f[k] if k == 3 else f[k]

    relay_up = push(window.at[5], window.at[4 + 2 * core], p_send, p_recv, 4, 4 + 2 * core, partner)
    relay_dn = push(window.at[1], window.at[2 * core], p_send, p_recv, 5, 2 * core, partner)

    def arrived(slot):
        push(params, window.at[slot], p_send, p_recv, 0, slot, partner).wait_recv()

    def pass_up():
        arrived(5)
        relay_up.start()

    def pass_dn():
        arrived(1)
        relay_dn.start()

    when_in(me + 2, pass_up)
    when_in(me - 2, pass_dn)
    for slot in (0, 2, 4, 6):
        when_in(me + slot - REACH, functools.partial(arrived, slot))
    own_copy.wait()
    state_copy.wait()

    rel = jnp.clip(offsets[0] - me + REACH, 0, REACH)
    for j in range(APER):
        b, c11, c13, c33, c44 = [window[rel + j, f] for f in range(5)]
        here = slice(j * slab, (j + 1) * slab)
        coef[0, here] = STEP_H * b
        coef[1, here] = STEP_H * c11
        coef[2, here] = STEP_H * c13
        coef[3, here] = STEP_H * c33
        coef[4, here] = STEP_H * c44
        coef[5, here] = (0.5 * STEP_H) * (c11 - c13)

    grad[...] = jnp.zeros_like(grad)

    @pl.loop(0, STEPS)
    def _(s):
        def velocity(i):
            hb = coef[0, i]
            sxx, syy, szz, sxy, sxz, syz = [state[3 + k, i] for k in range(6)]
            dxx = state[3, i + 1] - sxx if i + 1 < nx else -sxx
            dxy = sxy - state[6, i - 1] if i > 0 else sxy
            dxz = sxz - state[7, i - 1] if i > 0 else sxz
            vx = state[0, i] + hb * (dxx + bwd(sxy, 0) + bwd(sxz, 1))
            vy = state[1, i] + hb * (dxy + fwd(syy, 0) + bwd(syz, 1))
            vz = state[2, i] + hb * (dxz + bwd(syz, 0) + fwd(szz, 1)) + inject[s, i]
            state[0, i] = vx
            state[1, i] = vy
            state[2, i] = vz
            return vx, vy, vz

        def stress(i, before, here, after):
            vx, vy, vz = here
            exx, eyy, ezz, exy, exz, eyz = strains_at(
                here, None if before is None else before[0], None if after is None else after[1:]
            )
            h11, h13, h33, h44, h66 = [coef[k, i] for k in range(1, 6)]
            state[3, i] = state[3, i] + (h11 * exx + h13 * (eyy + ezz))
            state[4, i] = state[4, i] + (h11 * eyy + h13 * (exx + ezz))
            state[5, i] = state[5, i] + (h13 * (exx + eyy) + h33 * ezz)
            state[6, i] = state[6, i] + h66 * exy
            state[7, i] = state[7, i] + h44 * exz
            state[8, i] = state[8, i] + h44 * eyz
            fxx, fyy, fzz, fxy, fxz, fyz = [fstrain[s, k, i] for k in range(6)]
            ux, uy, uz = [snaps[s, c, i].astype(jnp.float32) for c in range(3)]
            shear = exy * fxy
            grad[0, i] = grad[0, i] + (vx * ux + vy * uy + vz * uz)
            grad[1, i] = grad[1, i] + (exx * fxx + eyy * fyy + shear)
            grad[2, i] = grad[2, i] + (
                exx * (fyy + fzz) + eyy * (fxx + fzz) + ezz * (fxx + fyy) - shear
            )
            grad[3, i] = grad[3, i] + ezz * fzz
            grad[4, i] = grad[4, i] + (exz * fxz + eyz * fyz)

        before, here = None, velocity(0)
        for i in range(nx):
            after = velocity(i + 1) if i + 1 < nx else None
            stress(i, before, here, after)
            before, here = here, after

    source = sources[0, 0]
    sx = lax.div(source, ny * nz)
    sy = lax.rem(lax.div(source, nz), ny)
    sz = lax.rem(source, nz)
    dy = lax.broadcasted_iota(jnp.int32, (ny, nz), 0) - sy
    dz = lax.broadcasted_iota(jnp.int32, (ny, nz), 1) - sz
    flat = dy * dy + dz * dz
    for i in range(nx):
        dx = i - sx
        d2 = (flat + dx * dx).astype(jnp.float32)
        weight = d2 / (d2 + float(MUTE * MUTE))
        for f in range(5):
            grad[f, i] = grad[f, i] * weight

    def place(pos):
        j = pos - rel
        ok = jnp.logical_and(j >= 0, j < APER)
        start = slab * jnp.clip(j, 0, APER - 1)
        for f in range(5):
            for k in range(slab):
                gwin[pos, f, k] = jnp.where(ok, grad[f, start + k], 0.0)

    for pos in range(SPAN):
        place(pos)

    to_pair = [
        push(gwin.at[2 * (1 - core) + 2 * j], fromp.at[j], g_send, g_recv, j, j, partner)
        for j in range(3)
    ]
    to_far = push(gwin.at[6 * core], landed.at[2], g_send, g_recv, 3, 5, far)
    when_in(far, to_far.start)
    for j in (2, 0, 1):
        to_pair[j].start()
    to_up = push(sumbuf.at[0], landed.at[0], g_send, g_recv, 4, 3, me + 2)
    to_dn = push(sumbuf.at[1], landed.at[1], g_send, g_recv, 5, 4, me - 2)
    to_pair[2].wait_recv()
    sumbuf[0] = gwin[5] + fromp[2]
    when_in(me + 2, to_up.start)
    to_pair[0].wait_recv()
    sumbuf[1] = gwin[1] + fromp[0]
    when_in(me - 2, to_dn.start)
    to_pair[1].wait_recv()
    out[...] = gwin[REACH] + fromp[1]

    def add_landed(k, sem):
        def go():
            push(sumbuf.at[0], landed.at[k], g_send, g_recv, 0, sem, partner).wait_recv()
            out[...] += landed[k]

        return go

    when_in(me - 2, add_landed(0, 3))
    when_in(me + 2, add_landed(1, 4))
    when_in(far, add_landed(2, 5))

    for f in range(5):
        biggest = jnp.max(jnp.abs(out[f]))
        mine[f : f + 1, :] = jnp.full((1, 128), biggest, jnp.float32)
    mine[5:8, :] = jnp.zeros((3, 128), jnp.float32)

    def max_copy(d):
        to = lax.rem(me + d, tiles)
        return push(mine, maxima.at[d - 1], m_send, m_recv, d - 1, d - 1, to)

    @pl.loop(1, tiles)
    def _(d):
        max_copy(d).start()

    def take(d, largest):
        max_copy(d).wait_recv()
        return jnp.maximum(largest, maxima[d - 1])

    largest = lax.fori_loop(1, tiles, take, mine[...])
    scale = 1.0 / (largest + EPSILON)
    for f in range(5):
        row = jnp.concatenate([scale[f : f + 1, :]] * (nz // 128), axis=1)
        out[f] = out[f] * row

    when_in(me + 2, send_up.wait_send)
    when_in(me - 2, send_dn.wait_send)
    when_in(far, send_far.wait_send)
    send_pa.wait_send()
    when_in(me + 2, relay_up.wait_send)
    when_in(me - 2, relay_dn.wait_send)
    for j in range(3):
        to_pair[j].wait_send()
    when_in(far, to_far.wait_send)
    when_in(me + 2, to_up.wait_send)
    when_in(me - 2, to_dn.wait_send)

    @pl.loop(1, tiles)
    def _(d):
        max_copy(d).wait_send()


def on_device(params, adjoint_state, snapshots, residuals, receivers, sources, offsets):
    tiles = lax.axis_size("tile")
    grid = adjoint_state.shape[3:]
    slab_shape = params.shape
    f32 = jnp.float32
    any_spec = pl.BlockSpec(memory_space=pl.ANY)
    smem = pl.BlockSpec(memory_space=pltpu.SMEM)
    vmem = pl.BlockSpec(memory_space=pltpu.VMEM)
    dma = pltpu.SemaphoreType.DMA
    return pl.pallas_call(
        functools.partial(kernel, tiles),
        out_shape=jax.ShapeDtypeStruct(slab_shape, f32),
        in_specs=[smem, smem, any_spec, any_spec, any_spec, vmem, vmem],
        out_specs=vmem,
        scratch_shapes=[
            pltpu.VMEM((SPAN,) + slab_shape, f32),
            pltpu.VMEM((9,) + grid, f32),
            pltpu.VMEM((STEPS, 3) + grid, jnp.bfloat16),
            pltpu.VMEM((STEPS,) + grid, f32),
            pltpu.VMEM((STEPS, 6) + grid, f32),
            pltpu.VMEM((6,) + grid, f32),
            pltpu.VMEM((5,) + grid, f32),
            pltpu.VMEM((SPAN,) + slab_shape, f32),
            pltpu.VMEM((3,) + slab_shape, f32),
            pltpu.VMEM((2,) + slab_shape, f32),
            pltpu.VMEM((3,) + slab_shape, f32),
            pltpu.VMEM((8, 128), f32),
            pltpu.VMEM((tiles - 1, 8, 128), f32),
            dma((3,)),
            dma((6,)),
            dma((SPAN,)),
            dma((6,)),
            dma((6,)),
            dma((tiles - 1,)),
            dma((tiles - 1,)),
        ],
        compiler_params=pltpu.CompilerParams(
            collective_id=0, has_side_effects=True, vmem_limit_bytes=40 * 1024 * 1024
        ),
    )(offsets, sources, params, adjoint_state, snapshots, residuals, receivers[0])


def solution(mesh):
    placed = (
        P("groups", "tile", None, None),
        P("tile", "groups", None, None, None, None),
        P("tile", "groups", None, None, None, None, None),
        P("tile", "groups", None, None),
        P("tile", "groups", None),
        P("tile", "groups"),
        P("tile"),
    )
    return jax.shard_map(
        on_device,
        mesh=mesh,
        in_specs=placed,
        out_specs=P("groups", "tile", None, None),
        check_vma=False,
    )
```

time: 208 us -> 41.2 us (0.20)
  local copies, waits for them, and re-layouts: 79 us -> 5.5 us
  other arithmetic: 52.8 us -> 0 us
  blocking collectives: 35.8 us -> 0 us
  Pallas kernels: 0 us -> 34.2 us
  starting transfers between devices: 32.1 us -> 0 us
  waiting for transfers between devices: 3.19 us -> 0 us
  between operations: 3.65 us -> 1.31 us
    slice x112 -> x0, local copies, waits for them, and re-layouts: 65 us -> none  [the longest x88 51.8 us: forward_diff(): shifted = lax.slice_in_dim(wavefield, 1, length, axis=along)]
    pmax x1 -> x0, blocking collectives: 35.8 us -> none  [on_device(): largest = lax.pmax(largest, 'tile')]
    pallas_call x0 -> x1, Pallas kernels: none -> 34.2 us  [on_device(): pl.pallas_call(functools.partial(kernel, tiles), out_shape=jax.ShapeDtype...]
    ppermute x12 -> x0, starting transfers between devices: 32.1 us -> none  [passed_along(): return lax.ppermute(shard, axis, pairs)]
    add x25 -> x0, other arithmetic: 22.3 us -> none  [the longest x4 8.86 us: shot_gradient(): stress_xz = stress_xz + STEP_H * stiff_44 * strain_xz]
    scatter-add x6 -> x0, other arithmetic: 12.3 us -> none  [shot_gradient(): velocity_z.reshape(-1).at[receiver].add(residual[step_index])]
    unnamed x4 -> x0, other arithmetic: 8.63 us -> none
    unnamed x318 -> x10, local copies, waits for them, and re-layouts: 11 us -> 5.5 us
  transfers between devices with their start and end apart: 12 -> 0, of which waited for: 2 -> 0; matrix products, arithmetic and copies ran while one was open for 20% -> 0% of each run, Pallas kernels for 0% -> 0%
where the time goes in v1:
time: 41.2 us; the launch traced here: 41 us
  Pallas kernels  34.2 us (83%)
  local copies, waits for them, and re-layouts  5.5 us (13%)
  between operations  1.31 us (3%)
    pallas_call x1, Pallas kernels, on_device(): pl.pallas_call(functools.partial(kernel, tiles), out_shape=jax.ShapeDtype...  34.2 us
    unnamed x10, local copies, waits for them, and re-layouts  5.5 us

profile of v1, /device:TPU:0, one launch (start us, length us, event | category | flops | bytes accessed | tf_op | source)
XLA Modules:
  0.0 41.0 jit_solution(11607224701089494672)
XLA Ops:
  1.3 0.7 %copy.8.residuals = f32[1,1,6,256]{3,2,1,0:T(8,128)S(1)} copy(f32[1,1,6,256]{3,1,2,0:T(1,128)} %param.10) | data formatting | bytes 12288 | tf_op args[3]
  2.0 0.0 copy-start
  2.0 1.3 %copy-done = f32[1,1,9,8,16,256]{5,4,3,2,1,0:T(8,128)S(1)} copy-done((f32[1,1,9,8,16,256]{5,4,3,2,1,0:T(8,128)S(1)}, f32[1,1,9,8,16,256]{5,4,3,2,1,0:T(8,128)}, u32[]{:S(2)}) %copy-start) | copy-done | bytes 1179672
  3.3 0.0 copy-start.1
  3.3 1.3 %copy-done.1 = bf16[1,1,6,3,8,16,256]{6,5,4,3,2,1,0:T(8,128)(2,1)S(1)} copy-done((bf16[1,1,6,3,8,16,256]{6,5,4,3,2,1,0:T(8,128)(2,1)S(1)}, bf16[1,1,6,3,8,16,256]{6,5,4,3,2,1,0:T(8,128)(2,1)}, u32[]{:S(2)}) %copy-start.1) | copy-done | bytes 1179672
  4.5 0.0 copy-start.2
  4.5 0.9 %copy-done.2 = f32[5,2,16,256]{3,2,1,0:T(8,128)S(1)} copy-done((f32[5,2,16,256]{3,2,1,0:T(8,128)S(1)}, f32[5,2,16,256]{3,2,1,0:T(8,128)}, u32[]{:S(2)}) %copy-start.2) | copy-done | bytes 163864
  5.5 0.0 copy-start.3
  5.5 0.7 %copy-done.3 = s32[1,1,256]{2,1,0:T(1,128)S(1)} copy-done((s32[1,1,256]{2,1,0:T(1,128)S(1)}, s32[1,1,256]{2,1,0:T(1,128)}, u32[]{:S(2)}) %copy-start.3) | copy-done | bytes 1048
  6.1 34.2 %shard_map.73 = f32[5,2,16,256]{3,2,1,0:T(8,128)S(1)} custom-call(s32[1]{0:T(128)S(6)} %copy.11.offsets, s32[1,1]{1,0:T(1,128)S(6)} %copy.10.sources, f32[5,2,16,256]{3,2,1,0:T(8,128)S(1)} %copy-done.2, f32[1,1,9,8,16,256]{5,4,3,2,1,0:T(8,128)S(1)} %copy-done, bf16[1,1,6,3,8,16,256]{6,5,4,3,2,1,0:T(8,128)(2,1)S(1)} %copy-done.1, ...), custom_call_target="tpu_custom_call" | custom-call | tf_op jit(solution)/shard_map/pallas_call | solution.py:353
  40.3 0.7 %copy.12 = f32[5,2,16,256]{3,2,1,0:T(8,128)} copy(f32[5,2,16,256]{3,2,1,0:T(8,128)S(1)} %shard_map.73) | data formatting | bytes 327680
Async XLA Ops:
  2.0 1.3 %copy-start = (f32[1,1,9,8,16,256]{5,4,3,2,1,0:T(8,128)S(1)}, f32[1,1,9,8,16,256]{5,4,3,2,1,0:T(8,128)}, u32[]{:S(2)}) copy-start(f32[1,1,9,8,16,256]{5,4,3,2,1,0:T(8,128)} %adjoint.1) | copy-start | bytes 3538948
  3.3 1.3 %copy-start.1 = (bf16[1,1,6,3,8,16,256]{6,5,4,3,2,1,0:T(8,128)(2,1)S(1)}, bf16[1,1,6,3,8,16,256]{6,5,4,3,2,1,0:T(8,128)(2,1)}, u32[]{:S(2)}) copy-start(bf16[1,1,6,3,8,16,256]{6,5,4,3,2,1,0:T(8,128)(2,1)} %snapshots.1) | copy-start | bytes 3538948
  4.5 0.9 %copy-start.2 = (f32[5,2,16,256]{3,2,1,0:T(8,128)S(1)}, f32[5,2,16,256]{3,2,1,0:T(8,128)}, u32[]{:S(2)}) copy-start(f32[5,2,16,256]{3,2,1,0:T(8,128)} %params.1) | copy-start | bytes 491524
  5.5 0.7 %copy-start.3 = (s32[1,1,256]{2,1,0:T(1,128)S(1)}, s32[1,1,256]{2,1,0:T(1,128)}, u32[]{:S(2)}) copy-start(s32[1,1,256]{2,1,0:T(1,128)} %param.11) | copy-start | bytes 3076

commit v2 on v1

v2 whole, which is shorter than its diff:
```python
import functools

import jax
import jax.numpy as jnp
from jax import lax
from jax.experimental import pallas as pl
from jax.experimental.pallas import tpu as pltpu
from jax.sharding import PartitionSpec as P

STEPS = 6
APER = 4
REACH = 3
MUTE = 4
SPAN = 2 * REACH + 1

STEP_H = 0.2
EPSILON = 1e-06
MESH = pl.DeviceIdType.MESH


def shift(blocks, axis, by):
    rows, columns = len(blocks), len(blocks[0])
    size = blocks[0][0].shape[axis]
    place = lax.broadcasted_iota(jnp.int32, blocks[0][0].shape, axis)
    edge = place == (size - 1 if by == 1 else 0)
    turn = size - 1 if by == 1 else 1
    rolled = [[pltpu.roll(b, turn, axis) for b in row] for row in blocks]

    def beyond(r, c):
        if axis == 0:
            r += by
        else:
            c += by
        return rolled[r][c] if 0 <= r < rows and 0 <= c < columns else 0.0

    return [
        [jnp.where(edge, beyond(r, c), rolled[r][c]) for c in range(columns)] for r in range(rows)
    ]


def per_block(fn, *planes):
    return [[fn(*cells) for cells in zip(*rows)] for rows in zip(*planes)]


def add(a, b):
    return per_block(lambda x, y: x + y, a, b)


def sub(a, b):
    return per_block(lambda x, y: x - y, a, b)


def mul(a, b):
    return per_block(lambda x, y: x * y, a, b)


def fwd(plane, axis):
    return sub(shift(plane, axis, 1), plane)


def bwd(plane, axis):
    return sub(plane, shift(plane, axis, -1))


def read(ref, *at):
    ny, nz = ref.shape[-2:]
    return [[ref[(*at, pl.ds(r, 8), pl.ds(c, 128))] for c in range(0, nz, 128)] for r in range(0, ny, 8)]


def write(ref, plane, *at):
    for r, row in enumerate(plane):
        for c, block in enumerate(row):
            ref[(*at, pl.ds(8 * r, 8), pl.ds(128 * c, 128))] = block


def strains_at(here, before, after):
    vx, vy, vz = here
    exx = vx if before is None else sub(vx, before)
    eyy = bwd(vy, 0)
    ezz = bwd(vz, 1)
    if after is None:
        exy = sub(fwd(vx, 0), vy)
        exz = sub(fwd(vx, 1), vz)
    else:
        exy = add(fwd(vx, 0), sub(after[0], vy))
        exz = add(fwd(vx, 1), sub(after[1], vz))
    eyz = add(fwd(vy, 1), fwd(vz, 0))
    return exx, eyy, ezz, exy, exz, eyz


def kernel(
    tiles,
    offsets,
    sources,
    params,
    adjoint,
    snapshots,
    residuals,
    receivers,
    out,
    window,
    state,
    snaps,
    resid,
    recs,
    inject,
    fields,
    coef,
    grad,
    gwin,
    fromp,
    sumbuf,
    landed,
    mine,
    maxima,
    local_sem,
    p_send,
    p_recv,
    g_send,
    g_recv,
    m_send,
    m_recv,
):
    me = lax.axis_index("tile")
    core = lax.rem(me, 2)
    xbit = lax.rem(lax.div(me, 2), 2)
    partner = me + 1 - 2 * core
    far = me + 3 * (2 * core - 1)
    xn = me + 2 - 4 * xbit
    zf = me + 4 - 8 * xbit
    zr = me - 4 + 8 * xbit
    nx = state.shape[1]
    nf, slab = params.shape[:2]
    ny, nz = state.shape[2], state.shape[3]

    barrier = pltpu.get_barrier_semaphore()

    @pl.loop(1, tiles)
    def _(d):
        pl.semaphore_signal(
            barrier, inc=1, device_id={"tile": lax.rem(me + d, tiles)}, device_id_type=MESH
        )

    own_copy = pltpu.make_async_copy(params, window.at[REACH], local_sem.at[0])
    state_copy = pltpu.make_async_copy(adjoint.at[0, 0], state, local_sem.at[1])
    snap_copy = pltpu.make_async_copy(snapshots.at[0, 0], snaps, local_sem.at[2])
    resid_copy = pltpu.make_async_copy(residuals, resid, local_sem.at[3])
    recs_copy = pltpu.make_async_copy(receivers, recs, local_sem.at[4])
    for copy in (recs_copy, resid_copy, snap_copy, own_copy, state_copy):
        copy.start()
    pl.semaphore_wait(barrier, tiles - 1)

    def push(src, dst, send, recv, to):
        return pltpu.make_async_remote_copy(
            src_ref=src,
            dst_ref=dst,
            send_sem=send,
            recv_sem=recv,
            device_id={"tile": to},
            device_id_type=MESH,
        )

    def when_in(t, fn):
        pl.when(jnp.logical_and(t >= 0, t < tiles))(fn)

    slot_x = 5 - 4 * xbit
    slot_z = 1 + 4 * xbit
    to_core = 2 * core - 1

    def send_x(f):
        return push(params.at[f], window.at[slot_z, f], p_send.at[0], p_recv.at[f], xn)

    send_own = push(params, window.at[2 + 2 * core], p_send.at[1], p_recv.at[10], partner)
    send_far = push(params, window.at[6 - 6 * core], p_send.at[2], p_recv.at[11], far)
    for f in range(nf):
        send_x(f).start()
    send_own.start()
    when_in(far, send_far.start)

    def on_z(f):
        block = window.at[slot_x, f]
        return push(block, window.at[slot_z, f], p_send.at[3], p_recv.at[5 + f], zf)

    def relay_x(f):
        block = window.at[slot_x, f]
        return push(block, window.at[slot_x + to_core, f], p_send.at[4], p_recv.at[12], partner)

    def relay_z(f):
        block = window.at[slot_z, f]
        return push(block, window.at[slot_z + to_core, f], p_send.at[5], p_recv.at[13], partner)

    def got(block, sem):
        push(block, block, p_send.at[0], sem, partner).wait_recv()

    def gone(block, sem):
        push(block, block, sem, p_recv.at[0], partner).wait_send()

    recs_copy.wait()
    resid_copy.wait()
    cells = recs[...]
    lanes = cells.shape[1]
    rows = nx * ny
    row_hit = lax.broadcasted_iota(jnp.int32, (rows, lanes), 0) == lax.div(cells, nz)
    col_hit = lax.broadcasted_iota(jnp.int32, (nz, lanes), 0) == lax.rem(cells, nz)
    columns = jnp.where(col_hit, 1.0, 0.0).astype(jnp.bfloat16)
    for s in range(STEPS):
        rest = resid[s]
        total = None
        for part in range(3):
            piece = rest.astype(jnp.bfloat16).astype(jnp.float32)
            rest = rest - piece
            left = jnp.where(row_hit, piece, 0.0).astype(jnp.bfloat16)
            term = lax.dot_general(
                left, columns, (((1,), (1,)), ((), ())), preferred_element_type=jnp.float32
            )
            total = term if total is None else total + term
        inject[s] = total.reshape(nx, ny, nz)

    snap_copy.wait()

    @pl.loop(0, STEPS)
    def _(s):
        @pl.when(s < nf)
        def _():
            got(window.at[slot_x, s], p_recv.at[s])
            when_in(zf, lambda: on_z(s).start())
            relay_x(s).start()

        def velocity(i):
            planes = []
            for c in range(3):
                u = snaps[s, c, i].astype(jnp.float32)
                blocks = [[u[r : r + 8, k : k + 128] for k in range(0, nz, 128)] for r in range(0, ny, 8)]
                planes.append(blocks)
                write(fields, blocks, s, 7 + c, i)
            return planes

        before, here = None, velocity(0)
        for i in range(nx):
            after = velocity(i + 1) if i + 1 < nx else None
            f = strains_at(
                here, None if before is None else before[0], None if after is None else after[1:]
            )
            fxx, fyy, fzz, fxy, fxz, fyz = f
            half = per_block(lambda x: 0.5 * x, fxy)
            trace = add(add(fxx, fyy), fzz)
            for k, plane in enumerate((fxx, fyy, fzz, half, fxz, fyz, trace)):
                write(fields, plane, s, k, i)
            before, here = here, after

    @pl.loop(0, nf)
    def _(f):
        def go():
            got(window.at[slot_z, f], p_recv.at[5 + f])
            relay_z(f).start()

        when_in(zr, go)

    got(window.at[4 - 2 * core], p_recv.at[10])
    when_in(far, lambda: got(window.at[6 * core], p_recv.at[11]))
    got(window.at[slot_x - to_core], p_recv.at[12])
    when_in(zr, lambda: got(window.at[slot_z - to_core], p_recv.at[13]))
    own_copy.wait()
    state_copy.wait()

    rel = jnp.clip(offsets[0] - me + REACH, 0, REACH)
    for j in range(APER):
        b, c11, c13, c33, c44 = [window[rel + j, f] for f in range(5)]
        here = slice(j * slab, (j + 1) * slab)
        coef[0, here] = STEP_H * b
        coef[1, here] = STEP_H * c13
        coef[2, here] = STEP_H * (c11 - c13)
        coef[3, here] = STEP_H * (c33 - c13)
        coef[4, here] = STEP_H * c44
        coef[5, here] = (0.5 * STEP_H) * (c11 - c13)

    grad[...] = jnp.zeros_like(grad)

    @pl.loop(0, STEPS)
    def _(s):
        def velocity(i):
            hb = read(coef, 0, i)
            sxx, syy, szz, sxy, sxz, syz = [read(state, 3 + k, i) for k in range(6)]
            if i + 1 < nx:
                dxx = sub(read(state, 3, i + 1), sxx)
            else:
                dxx = per_block(lambda x: -x, sxx)
            dxy = sub(sxy, read(state, 6, i - 1)) if i > 0 else sxy
            dxz = sub(sxz, read(state, 7, i - 1)) if i > 0 else sxz
            ax = add(dxx, add(bwd(sxy, 0), bwd(sxz, 1)))
            ay = add(dxy, add(fwd(syy, 0), bwd(syz, 1)))
            az = add(dxz, add(bwd(syz, 0), fwd(szz, 1)))
            vx = add(read(state, 0, i), mul(hb, ax))
            vy = add(read(state, 1, i), mul(hb, ay))
            vz = add(add(read(state, 2, i), read(inject, s, i)), mul(hb, az))
            for k, v in enumerate((vx, vy, vz)):
                write(state, v, k, i)

        def grow(ref, plane, *at):
            write(ref, add(read(ref, *at), plane), *at)

        def stress(i):
            here = [read(state, k, i) for k in range(3)]
            vx, vy, vz = here
            exx, eyy, ezz, exy, exz, eyz = strains_at(
                here,
                read(state, 0, i - 1) if i > 0 else None,
                [read(state, k, i + 1) for k in (1, 2)] if i + 1 < nx else None,
            )
            h13, d11, d33, h44, h66 = [read(coef, k, i) for k in range(1, 6)]
            trace = add(add(exx, eyy), ezz)
            common = mul(h13, trace)
            grow(state, add(common, mul(d11, exx)), 3, i)
            grow(state, add(common, mul(d11, eyy)), 4, i)
            grow(state, add(common, mul(d33, ezz)), 5, i)
            grow(state, mul(h66, exy), 6, i)
            grow(state, mul(h44, exz), 7, i)
            grow(state, mul(h44, eyz), 8, i)
            fxx, fyy, fzz, fxy, fxz, fyz, ftrace, ux, uy, uz = [read(fields, s, k, i) for k in range(10)]
            grow(grad, add(add(mul(vx, ux), mul(vy, uy)), mul(vz, uz)), 0, i)
            grow(grad, add(add(mul(exx, fxx), mul(eyy, fyy)), mul(exy, fxy)), 1, i)
            grow(grad, mul(trace, ftrace), 2, i)
            grow(grad, mul(ezz, fzz), 3, i)
            grow(grad, add(mul(exz, fxz), mul(eyz, fyz)), 4, i)

        velocity(0)
        for i in range(nx):
            if i + 1 < nx:
                velocity(i + 1)
            stress(i)

    source = sources[0, 0]
    sx = lax.div(source, ny * nz)
    sy = lax.rem(lax.div(source, nz), ny)
    sz = lax.rem(source, nz)
    dy = lax.broadcasted_iota(jnp.int32, (ny, nz), 0) - sy
    dz = lax.broadcasted_iota(jnp.int32, (ny, nz), 1) - sz
    flat = dy * dy + dz * dz
    for i in range(nx):
        dx = i - sx
        d2 = (flat + dx * dx).astype(jnp.float32)
        weight = d2 / (d2 + float(MUTE * MUTE))
        k11, k33 = grad[1, i], grad[3, i]
        grad[2, i] = (grad[2, i] - k11 - k33) * weight
        grad[1, i] = k11 * weight
        grad[3, i] = k33 * weight
        grad[0, i] = grad[0, i] * weight
        grad[4, i] = grad[4, i] * weight

    def place(pos):
        j = pos - rel
        ok = jnp.logical_and(j >= 0, j < APER)
        start = slab * jnp.clip(j, 0, APER - 1)
        for f in range(5):
            for k in range(slab):
                gwin[pos, f, k] = jnp.where(ok, grad[f, start + k], 0.0)

    pair = [
        push(gwin.at[pos - to_core], fromp.at[k], g_send.at[k], g_recv.at[10 + k], partner)
        for k, pos in enumerate((slot_z, slot_x, REACH))
    ]
    to_far = push(gwin.at[6 * core], landed.at[2], g_send.at[5], g_recv.at[13], far)
    for k, pos in enumerate((slot_z, slot_x, REACH)):
        place(pos - to_core)
        pair[k].start()
    place(slot_z)
    place(6 * core)
    place(slot_x)
    place(REACH)

    def to_z(f):
        return push(sumbuf.at[0, f], landed.at[0, f], g_send.at[3], g_recv.at[5 + f], zr)

    def to_x(f):
        return push(sumbuf.at[1, f], landed.at[1, f], g_send.at[4], g_recv.at[f], xn)

    pair[0].wait_recv()
    for f in range(nf):
        sumbuf[0, f] = gwin[slot_z, f] + fromp[0, f]
        when_in(zr, to_z(f).start)
    when_in(far, to_far.start)
    pair[1].wait_recv()
    for f in range(nf):
        sumbuf[1, f] = gwin[slot_x, f] + fromp[1, f]

        def join(f=f):
            got(landed.at[0, f], g_recv.at[5 + f])
            sumbuf[1, f] += landed[0, f]

        when_in(zf, join)
        to_x(f).start()
    pair[2].wait_recv()
    out[...] = gwin[REACH] + fromp[2]

    def join_far():
        got(landed.at[2], g_recv.at[13])
        out[...] += landed[2]

    when_in(far, join_far)

    for f in range(nf):
        got(landed.at[1, f], g_recv.at[f])
        total = out[f] + landed[1, f]
        out[f] = total
        biggest = jnp.max(jnp.abs(total), axis=(0, 1, 2), keepdims=True)
        mine[f : f + 1, :] = jnp.broadcast_to(biggest[0], (1, 128))
    mine[nf:8, :] = jnp.zeros((8 - nf, 128), jnp.float32)

    def max_copy(d):
        to = lax.rem(me + d, tiles)
        return push(mine, maxima.at[d - 1], m_send.at[d - 1], m_recv.at[d - 1], to)

    @pl.loop(1, tiles)
    def _(d):
        max_copy(d).start()

    gone(params, p_send.at[0])
    send_own.wait_send()
    when_in(far, send_far.wait_send)
    when_in(zf, lambda: gone(window.at[slot_x], p_send.at[3]))
    gone(window.at[slot_x], p_send.at[4])
    when_in(zr, lambda: gone(window.at[slot_z], p_send.at[5]))
    for copy in pair:
        copy.wait_send()
    when_in(far, to_far.wait_send)
    when_in(zr, lambda: gone(sumbuf.at[0], g_send.at[3]))
    gone(sumbuf.at[1], g_send.at[4])

    def take(d, largest):
        max_copy(d).wait_recv()
        return jnp.maximum(largest, maxima[d - 1])

    largest = lax.fori_loop(1, tiles, take, mine[...])
    scale = 1.0 / (largest + EPSILON)
    for f in range(nf):
        row = jnp.concatenate([scale[f : f + 1, :]] * (nz // 128), axis=1)
        out[f] = out[f] * row

    @pl.loop(1, tiles)
    def _(d):
        max_copy(d).wait_send()


def on_device(params, adjoint_state, snapshots, residuals, receivers, sources, offsets):
    tiles = lax.axis_size("tile")
    grid = adjoint_state.shape[3:]
    slab_shape = params.shape
    f32 = jnp.float32
    hbm = pl.BlockSpec(memory_space=pltpu.HBM)
    smem = pl.BlockSpec(memory_space=pltpu.SMEM)
    vmem = pl.BlockSpec(memory_space=pltpu.VMEM)
    dma = pltpu.SemaphoreType.DMA
    rows = jnp.transpose(residuals[0], (1, 0, 2))
    return pl.pallas_call(
        functools.partial(kernel, tiles),
        out_shape=jax.ShapeDtypeStruct(slab_shape, f32),
        in_specs=[smem, smem, hbm, hbm, hbm, hbm, hbm],
        out_specs=vmem,
        scratch_shapes=[
            pltpu.VMEM((SPAN,) + slab_shape, f32),
            pltpu.VMEM((9,) + grid, f32),
            pltpu.VMEM((STEPS, 3) + grid, jnp.bfloat16),
            pltpu.VMEM(rows.shape, f32),
            pltpu.VMEM(receivers.shape[1:], jnp.int32),
            pltpu.VMEM((STEPS,) + grid, f32),
            pltpu.VMEM((STEPS, 10) + grid, f32),
            pltpu.VMEM((6,) + grid, f32),
            pltpu.VMEM((5,) + grid, f32),
            pltpu.VMEM((SPAN,) + slab_shape, f32),
            pltpu.VMEM((3,) + slab_shape, f32),
            pltpu.VMEM((2,) + slab_shape, f32),
            pltpu.VMEM((3,) + slab_shape, f32),
            pltpu.VMEM((8, 128), f32),
            pltpu.VMEM((tiles - 1, 8, 128), f32),
            dma((5,)),
            dma((6,)),
            dma((14,)),
            dma((6,)),
            dma((14,)),
            dma((tiles - 1,)),
            dma((tiles - 1,)),
        ],
        compiler_params=pltpu.CompilerParams(
            collective_id=0, has_side_effects=True, vmem_limit_bytes=56 * 1024 * 1024
        ),
    )(offsets, sources, params, adjoint_state, snapshots, rows, receivers[0])


def solution(mesh):
    placed = (
        P("groups", "tile", None, None),
        P("tile", "groups", None, None, None, None),
        P("tile", "groups", None, None, None, None, None),
        P("tile", "groups", None, None),
        P("tile", "groups", None),
        P("tile", "groups"),
        P("tile"),
    )
    return jax.shard_map(
        on_device,
        mesh=mesh,
        in_specs=placed,
        out_specs=P("groups", "tile", None, None),
        check_vma=False,
    )
```

time: 41.2 us -> 36.6 us (0.89)
  local copies, waits for them, and re-layouts: 5.5 us -> 1.59 us
  Pallas kernels: 34.2 us -> 33.6 us
    unnamed x10 -> x1, local copies, waits for them, and re-layouts: 5.5 us -> 1.59 us
    pallas_call x1, Pallas kernels: 34.2 us -> 33.6 us  [on_device(): pl.pallas_call(functools.partial(kernel, tiles), out_shape=jax.ShapeDtype...]
where the time goes in v2:
time: 36.6 us; the launch traced here: 36.5 us
  Pallas kernels  33.6 us (92%)
  local copies, waits for them, and re-layouts  1.59 us (4%)
  between operations  1.3 us (4%)
    pallas_call x1, Pallas kernels, on_device(): pl.pallas_call(functools.partial(kernel, tiles), out_shape=jax.ShapeDtype...  33.6 us
    unnamed x1, local copies, waits for them, and re-layouts  1.59 us

profile of v2, /device:TPU:0, one launch (start us, length us, event | category | flops | bytes accessed | tf_op | source)
XLA Modules:
  0.0 36.5 jit_solution(8301331121845893416)
XLA Ops:
  1.3 33.6 %shard_map.73 = f32[5,2,16,256]{3,2,1,0:T(8,128)} custom-call(s32[1]{0:T(128)S(6)} %copy.10.offsets, s32[1,1]{1,0:T(1,128)S(6)} %copy.9.sources, f32[5,2,16,256]{3,2,1,0:T(8,128)} %params.1, f32[1,1,9,8,16,256]{5,4,3,2,1,0:T(8,128)} %adjoint.1, bf16[1,1,6,3,8,16,256]{6,5,4,3,2,1,0:T(8,128)(2,1)} %snapshots.1, f32[6,1,256]{2,1,0:T(1,128)} %bitcast.2, ...), custom_call_target="tpu_custom_call" | custom-call | tf_op jit(solution)/shard_map/pallas_call | solution.py:454
  34.9 1.6 %copy.11 = f32[5,2,16,256]{3,2,1,0:T(8,128)} copy(f32[5,2,16,256]{3,2,1,0:T(8,128)} %shard_map.73) | data formatting | bytes 327680

commit v3 on v2

v3 whole, which is shorter than its diff:
```python
import functools

import jax
import jax.numpy as jnp
from jax import lax
from jax.experimental import pallas as pl
from jax.experimental.pallas import tpu as pltpu
from jax.sharding import PartitionSpec as P

STEPS = 6
APER = 4
REACH = 3
MUTE = 4
SPAN = 2 * REACH + 1

STEP_H = 0.2
EPSILON = 1e-06
MESH = pl.DeviceIdType.MESH


def shifted(blocks, axis, by):
    rows, columns = len(blocks), len(blocks[0])
    size = blocks[0][0].shape[axis]
    place = lax.broadcasted_iota(jnp.int32, blocks[0][0].shape, axis)
    edge = place == (size - 1 if by == 1 else 0)
    turn = size - 1 if by == 1 else 1
    rolled = [[pltpu.roll(b, turn, axis) for b in row] for row in blocks]

    def at(r, c):
        nr, nc = (r + by, c) if axis == 0 else (r, c + by)
        beyond = rolled[nr][nc] if 0 <= nr < rows and 0 <= nc < columns else 0.0
        return jnp.where(edge, beyond, rolled[r][c])

    return at


def block_of(r, c):
    return pl.ds(8 * r, 8), pl.ds(128 * c, 128)


def read(ref, *at):
    ny, nz = ref.shape[-2:]
    return [[ref[(*at, *block_of(r, c))] for c in range(nz // 128)] for r in range(ny // 8)]


def strains_of(here, before, after):
    vx, vy, vz = here
    vx_y, vx_z = shifted(vx, 0, 1), shifted(vx, 1, 1)
    vy_y, vy_z = shifted(vy, 0, -1), shifted(vy, 1, 1)
    vz_y, vz_z = shifted(vz, 0, 1), shifted(vz, 1, -1)

    def at(r, c):
        x, y, z = vx[r][c], vy[r][c], vz[r][c]
        exx = x if before is None else x - before(r, c)
        eyy = y - vy_y(r, c)
        ezz = z - vz_z(r, c)
        dy = -y if after is None else after[0](r, c) - y
        dz = -z if after is None else after[1](r, c) - z
        exy = (vx_y(r, c) - x) + dy
        exz = (vx_z(r, c) - x) + dz
        eyz = (vy_z(r, c) - y) + (vz_y(r, c) - z)
        return exx, eyy, ezz, exy, exz, eyz

    return at


def kernel(
    tiles,
    offsets,
    sources,
    params,
    adjoint,
    snapshots,
    residuals,
    receivers,
    summed,
    scales,
    out,
    offset,
    source_at,
    window,
    state,
    snaps,
    resid,
    recs,
    inject,
    fields,
    coef,
    grad,
    gwin,
    fromp,
    sumbuf,
    landed,
    mine,
    maxima,
    local_sem,
    p_send,
    p_recv,
    g_send,
    g_recv,
    m_send,
    m_recv,
):
    me = lax.axis_index("tile")
    core = lax.rem(me, 2)
    xbit = lax.rem(lax.div(me, 2), 2)
    partner = me + 1 - 2 * core
    far = me + 3 * (2 * core - 1)
    xn = me + 2 - 4 * xbit
    zf = me + 4 - 8 * xbit
    zr = me - 4 + 8 * xbit
    nx = state.shape[1]
    nf, slab = params.shape[:2]
    ny, nz = state.shape[2], state.shape[3]

    barrier = pltpu.get_barrier_semaphore()

    @pl.loop(1, tiles)
    def _(d):
        pl.semaphore_signal(
            barrier, inc=1, device_id={"tile": lax.rem(me + d, tiles)}, device_id_type=MESH
        )

    own_copy = pltpu.make_async_copy(params, window.at[REACH], local_sem.at[0])
    state_copy = pltpu.make_async_copy(adjoint.at[0, 0], state, local_sem.at[1])
    snap_copy = pltpu.make_async_copy(snapshots.at[0, 0], snaps, local_sem.at[2])
    resid_copy = pltpu.make_async_copy(residuals, resid, local_sem.at[3])
    recs_copy = pltpu.make_async_copy(receivers, recs, local_sem.at[4])
    offset_copy = pltpu.make_async_copy(offsets, offset, local_sem.at[5])
    source_copy = pltpu.make_async_copy(sources, source_at, local_sem.at[6])
    for copy in (recs_copy, resid_copy, snap_copy, own_copy, state_copy, offset_copy, source_copy):
        copy.start()
    pl.semaphore_wait(barrier, tiles - 1)

    def push(src, dst, send, recv, to):
        return pltpu.make_async_remote_copy(
            src_ref=src,
            dst_ref=dst,
            send_sem=send,
            recv_sem=recv,
            device_id={"tile": to},
            device_id_type=MESH,
        )

    def when_in(t, fn):
        pl.when(jnp.logical_and(t >= 0, t < tiles))(fn)

    slot_x = 5 - 4 * xbit
    slot_z = 1 + 4 * xbit
    to_core = 2 * core - 1

    def send_x(f):
        return push(params.at[f], window.at[slot_z, f], p_send.at[0], p_recv.at[f], xn)

    send_own = push(params, window.at[2 + 2 * core], p_send.at[1], p_recv.at[10], partner)
    send_far = push(params, window.at[6 - 6 * core], p_send.at[2], p_recv.at[11], far)
    for f in range(nf):
        send_x(f).start()
    send_own.start()
    when_in(far, send_far.start)

    def on_z(f):
        block = window.at[slot_x, f]
        return push(block, window.at[slot_z, f], p_send.at[3], p_recv.at[5 + f], zf)

    def relay_x(f):
        block = window.at[slot_x, f]
        return push(block, window.at[slot_x + to_core, f], p_send.at[4], p_recv.at[12], partner)

    def relay_z(f):
        block = window.at[slot_z, f]
        return push(block, window.at[slot_z + to_core, f], p_send.at[5], p_recv.at[13], partner)

    def got(block, sem):
        push(block, block, p_send.at[0], sem, partner).wait_recv()

    def gone(block, sem):
        push(block, block, sem, p_recv.at[0], partner).wait_send()

    recs_copy.wait()
    resid_copy.wait()
    snap_copy.wait()
    cells = recs[...]
    lanes = cells.shape[1]
    rows = nx * ny
    blocks = [(r, c) for r in range(ny // 8) for c in range(nz // 128)]

    def pass_z(f):
        def go():
            got(window.at[slot_z, f], p_recv.at[5 + f])
            relay_z(f).start()

        when_in(zr, go)

    @pl.loop(0, STEPS)
    def _(s):
        @pl.when(s < nf)
        def _():
            got(window.at[slot_x, s], p_recv.at[s])
            when_in(zf, lambda: on_z(s).start())
            relay_x(s).start()

        @pl.when(s >= 2)
        def _():
            pass_z(s - 2)

        def velocity(i):
            planes = []
            for c in range(3):
                u = snaps[s, c, i].astype(jnp.float32)
                fields[s, 7 + c, i] = u
                planes.append(
                    [[u[r : r + 8, k : k + 128] for k in range(0, nz, 128)] for r in range(0, ny, 8)]
                )
            return planes

        def picker(plane):
            return lambda r, c: plane[r][c]

        before, here = None, velocity(0)
        for i in range(nx):
            after = velocity(i + 1) if i + 1 < nx else None
            strains = strains_of(
                here,
                None if before is None else picker(before[0]),
                None if after is None else [picker(after[1]), picker(after[2])],
            )
            for r, c in blocks:
                fxx, fyy, fzz, fxy, fxz, fyz = strains(r, c)
                trace = fxx + fyy + fzz
                for k, value in enumerate((fxx, fyy, fzz, 0.5 * fxy, fxz, fyz, trace)):
                    fields[(s, k, i, *block_of(r, c))] = value
            before, here = here, after

        row_hit = lax.broadcasted_iota(jnp.int32, (rows, lanes), 0) == lax.div(cells, nz)
        col_hit = lax.broadcasted_iota(jnp.int32, (nz, lanes), 0) == lax.rem(cells, nz)
        columns = jnp.where(col_hit, 1.0, 0.0).astype(jnp.bfloat16)
        rest = resid[s]
        left = []
        for part in range(3):
            piece = rest.astype(jnp.bfloat16).astype(jnp.float32)
            rest = rest - piece
            left.append(jnp.where(row_hit, piece, 0.0).astype(jnp.bfloat16))
        terms = lax.dot_general(
            jnp.concatenate(left, axis=0),
            columns,
            (((1,), (1,)), ((), ())),
            preferred_element_type=jnp.float32,
        )
        total = terms[:rows] + (terms[rows : 2 * rows] + terms[2 * rows :])
        inject[s] = total.reshape(nx, ny, nz)

    pass_z(nf - 1)
    got(window.at[4 - 2 * core], p_recv.at[10])
    when_in(far, lambda: got(window.at[6 * core], p_recv.at[11]))
    got(window.at[slot_x - to_core], p_recv.at[12])
    when_in(zr, lambda: got(window.at[slot_z - to_core], p_recv.at[13]))
    own_copy.wait()
    state_copy.wait()

    offset_copy.wait()
    source_copy.wait()
    rel = jnp.clip(offset[0] - me + REACH, 0, REACH)
    for j in range(APER):
        b, c11, c13, c33, c44 = [window[rel + j, f] for f in range(5)]
        here = slice(j * slab, (j + 1) * slab)
        coef[0, here] = STEP_H * b
        coef[1, here] = STEP_H * c13
        coef[2, here] = STEP_H * (c11 - c13)
        coef[3, here] = STEP_H * (c33 - c13)
        coef[4, here] = STEP_H * c44
        coef[5, here] = (0.5 * STEP_H) * (c11 - c13)

    grad[...] = jnp.zeros_like(grad)

    @pl.loop(0, STEPS)
    def _(s):
        def velocity(i):
            sxy, sxz, syy, syz, szz = [read(state, k, i) for k in (6, 7, 4, 8, 5)]
            sxy_y, sxz_z = shifted(sxy, 0, -1), shifted(sxz, 1, -1)
            syy_y, syz_z = shifted(syy, 0, 1), shifted(syz, 1, -1)
            syz_y, szz_z = shifted(syz, 0, -1), shifted(szz, 1, 1)
            for r, c in blocks:
                at = block_of(r, c)
                hb = coef[(0, i, *at)]
                sxx = state[(3, i, *at)]
                xy, xz, yy, yz, zz = [f[r][c] for f in (sxy, sxz, syy, syz, szz)]
                dxx = state[(3, i + 1, *at)] - sxx if i + 1 < nx else -sxx
                dxy = xy - state[(6, i - 1, *at)] if i > 0 else xy
                dxz = xz - state[(7, i - 1, *at)] if i > 0 else xz
                ax = dxx + ((xy - sxy_y(r, c)) + (xz - sxz_z(r, c)))
                ay = dxy + ((syy_y(r, c) - yy) + (yz - syz_z(r, c)))
                az = dxz + ((yz - syz_y(r, c)) + (szz_z(r, c) - zz))
                state[(0, i, *at)] += hb * ax
                state[(1, i, *at)] += hb * ay
                state[(2, i, *at)] = (state[(2, i, *at)] + inject[(s, i, *at)]) + hb * az

        def stress(i):
            here = [read(state, k, i) for k in range(3)]

            def picker(k, plane):
                return lambda r, c: state[(k, plane, *block_of(r, c))]

            strains = strains_of(
                here,
                picker(0, i - 1) if i > 0 else None,
                [picker(1, i + 1), picker(2, i + 1)] if i + 1 < nx else None,
            )
            for r, c in blocks:
                at = block_of(r, c)
                vx, vy, vz = [v[r][c] for v in here]
                exx, eyy, ezz, exy, exz, eyz = strains(r, c)
                h13, d11, d33, h44, h66 = [coef[(k, i, *at)] for k in range(1, 6)]
                trace = exx + eyy + ezz
                common = h13 * trace
                state[(3, i, *at)] += common + d11 * exx
                state[(4, i, *at)] += common + d11 * eyy
                state[(5, i, *at)] += common + d33 * ezz
                state[(6, i, *at)] += h66 * exy
                state[(7, i, *at)] += h44 * exz
                state[(8, i, *at)] += h44 * eyz
                fxx, fyy, fzz, fxy, fxz, fyz, ftrace, ux, uy, uz = [
                    fields[(s, k, i, *at)] for k in range(10)
                ]
                grad[(0, i, *at)] += vx * ux + vy * uy + vz * uz
                grad[(1, i, *at)] += exx * fxx + eyy * fyy + exy * fxy
                grad[(2, i, *at)] += trace * ftrace
                grad[(3, i, *at)] += ezz * fzz
                grad[(4, i, *at)] += exz * fxz + eyz * fyz

        velocity(0)
        for i in range(nx):
            if i + 1 < nx:
                velocity(i + 1)
            stress(i)

    source = source_at[0, 0]
    sx = lax.div(source, ny * nz)
    sy = lax.rem(lax.div(source, nz), ny)
    sz = lax.rem(source, nz)
    dy = lax.broadcasted_iota(jnp.int32, (ny, nz), 0) - sy
    dz = lax.broadcasted_iota(jnp.int32, (ny, nz), 1) - sz
    flat = dy * dy + dz * dz
    for i in range(nx):
        dx = i - sx
        d2 = (flat + dx * dx).astype(jnp.float32)
        weight = d2 / (d2 + float(MUTE * MUTE))
        k11, k33 = grad[1, i], grad[3, i]
        grad[2, i] = (grad[2, i] - k11 - k33) * weight
        grad[1, i] = k11 * weight
        grad[3, i] = k33 * weight
        grad[0, i] = grad[0, i] * weight
        grad[4, i] = grad[4, i] * weight

    def place(pos):
        j = pos - rel
        ok = jnp.logical_and(j >= 0, j < APER)
        start = slab * jnp.clip(j, 0, APER - 1)
        for f in range(5):
            for k in range(slab):
                gwin[pos, f, k] = jnp.where(ok, grad[f, start + k], 0.0)

    pair = [
        push(gwin.at[pos - to_core], fromp.at[k], g_send.at[k], g_recv.at[10 + k], partner)
        for k, pos in enumerate((slot_z, slot_x, REACH))
    ]
    to_far = push(gwin.at[6 * core], landed.at[2], g_send.at[5], g_recv.at[13], far)
    for k, pos in enumerate((slot_z, slot_x, REACH)):
        place(pos - to_core)
        pair[k].start()
    place(slot_z)
    place(6 * core)
    place(slot_x)
    place(REACH)

    def to_z(f):
        return push(sumbuf.at[0, f], landed.at[0, f], g_send.at[3], g_recv.at[5 + f], zr)

    def to_x(f):
        return push(sumbuf.at[1, f], landed.at[1, f], g_send.at[4], g_recv.at[f], xn)

    pair[0].wait_recv()
    for f in range(nf):
        sumbuf[0, f] = gwin[slot_z, f] + fromp[0, f]
        when_in(zr, to_z(f).start)
    when_in(far, to_far.start)
    pair[1].wait_recv()
    for f in range(nf):
        sumbuf[1, f] = gwin[slot_x, f] + fromp[1, f]

        def join(f=f):
            got(landed.at[0, f], g_recv.at[5 + f])
            sumbuf[1, f] += landed[0, f]

        when_in(zf, join)
        to_x(f).start()
    pair[2].wait_recv()
    out[...] = gwin[REACH] + fromp[2]

    def join_far():
        got(landed.at[2], g_recv.at[13])
        out[...] += landed[2]

    when_in(far, join_far)

    lane = lax.broadcasted_iota(jnp.int32, (1, 128), 1)
    row = jnp.zeros((1, 128), jnp.float32)
    for f in range(nf):
        got(landed.at[1, f], g_recv.at[f])
        total = out[f] + landed[1, f]
        out[f] = total
        biggest = jnp.max(jnp.abs(total), axis=(0, 1, 2), keepdims=True)[0]
        row = jnp.where(lane == f, biggest, row)
    mine[...] = row

    def max_copy(d):
        to = lax.rem(me + d, tiles)
        return push(mine, maxima.at[d - 1], m_send.at[0], m_recv.at[0], to)

    @pl.loop(1, tiles)
    def _(d):
        max_copy(d).start()

    store = pltpu.make_async_copy(out, summed, local_sem.at[7])
    store.start()

    gone(params, p_send.at[0])
    send_own.wait_send()
    when_in(far, send_far.wait_send)
    when_in(zf, lambda: gone(window.at[slot_x], p_send.at[3]))
    gone(window.at[slot_x], p_send.at[4])
    when_in(zr, lambda: gone(window.at[slot_z], p_send.at[5]))
    for copy in pair:
        copy.wait_send()
    when_in(far, to_far.wait_send)
    when_in(zr, lambda: gone(sumbuf.at[0], g_send.at[3]))
    gone(sumbuf.at[1], g_send.at[4])

    got(maxima, m_recv.at[0])
    scale = 1.0 / (jnp.maximum(jnp.max(maxima[...], axis=0), row) + EPSILON)
    for f in range(nf):
        factor = jnp.sum(jnp.where(lane == f, scale, 0.0), axis=1, keepdims=True)
        scales[f] = jnp.broadcast_to(factor, (1, nz))
    gone(maxima, m_send.at[0])
    store.wait()


def on_device(params, adjoint_state, snapshots, residuals, receivers, sources, offsets):
    tiles = lax.axis_size("tile")
    grid = adjoint_state.shape[3:]
    slab_shape = params.shape
    f32 = jnp.float32
    hbm = pl.BlockSpec(memory_space=pltpu.HBM)
    vmem = pl.BlockSpec(memory_space=pltpu.VMEM)
    dma = pltpu.SemaphoreType.DMA
    rows = jnp.transpose(residuals[0], (1, 0, 2))
    summed, scales = pl.pallas_call(
        functools.partial(kernel, tiles),
        out_shape=[
            jax.ShapeDtypeStruct(slab_shape, f32),
            jax.ShapeDtypeStruct((slab_shape[0], 1, slab_shape[3]), f32),
        ],
        in_specs=[hbm, hbm, hbm, hbm, hbm, hbm, hbm],
        out_specs=[hbm, vmem],
        scratch_shapes=[
            pltpu.VMEM(slab_shape, f32),
            pltpu.SMEM(offsets.shape, jnp.int32),
            pltpu.SMEM(sources.shape, jnp.int32),
            pltpu.VMEM((SPAN,) + slab_shape, f32),
            pltpu.VMEM((9,) + grid, f32),
            pltpu.VMEM((STEPS, 3) + grid, jnp.bfloat16),
            pltpu.VMEM(rows.shape, f32),
            pltpu.VMEM(receivers.shape[1:], jnp.int32),
            pltpu.VMEM((STEPS,) + grid, f32),
            pltpu.VMEM((STEPS, 10) + grid, f32),
            pltpu.VMEM((6,) + grid, f32),
            pltpu.VMEM((5,) + grid, f32),
            pltpu.VMEM((SPAN,) + slab_shape, f32),
            pltpu.VMEM((3,) + slab_shape, f32),
            pltpu.VMEM((2,) + slab_shape, f32),
            pltpu.VMEM((3,) + slab_shape, f32),
            pltpu.VMEM((1, 128), f32),
            pltpu.VMEM((tiles - 1, 1, 128), f32),
            dma((8,)),
            dma((6,)),
            dma((14,)),
            dma((6,)),
            dma((14,)),
            dma((1,)),
            dma((1,)),
        ],
        compiler_params=pltpu.CompilerParams(
            collective_id=0, has_side_effects=True, vmem_limit_bytes=56 * 1024 * 1024
        ),
    )(offsets, sources, params, adjoint_state, snapshots, rows, receivers[0])
    return summed * scales[:, :, None, :]


def solution(mesh):
    placed = (
        P("groups", "tile", None, None),
        P("tile", "groups", None, None, None, None),
        P("tile", "groups", None, None, None, None, None),
        P("tile", "groups", None, None),
        P("tile", "groups", None),
        P("tile", "groups"),
        P("tile"),
    )
    return jax.shard_map(
        on_device,
        mesh=mesh,
        in_specs=placed,
        out_specs=P("groups", "tile", None, None),
        check_vma=False,
    )
```

time: 36.6 us -> 38.2 us (1.044)
  other arithmetic: 0 us -> 1.6 us
  local copies, waits for them, and re-layouts: 1.59 us -> 0.69 us
  Pallas kernels: 33.6 us -> 34.4 us
    mul x0 -> x1, other arithmetic: none -> 1.6 us  [on_device(): return summed * scales[:, :, None, :]]
    unnamed x1, local copies, waits for them, and re-layouts: 1.59 us -> 0.69 us
    pallas_call x1, Pallas kernels: 33.6 us -> 34.4 us  [on_device(): pl.pallas_call(functools.partial(kernel, tiles), out_shape=[jax.ShapeDtyp...]
where the time goes in v3:
time: 38.2 us; the launch traced here: 38 us
  Pallas kernels  34.4 us (90%)
  other arithmetic  1.6 us (4%)
  between operations  1.31 us (3%)
  local copies, waits for them, and re-layouts  0.69 us (2%)
    pallas_call x1, Pallas kernels, on_device(): pl.pallas_call(functools.partial(kernel, tiles), out_shape=[jax.ShapeDtyp...  34.4 us
    mul x1, other arithmetic, on_device(): return summed * scales[:, :, None, :]  1.6 us

profile of v3, /device:TPU:0, one launch (start us, length us, event | category | flops | bytes accessed | tf_op | source)
XLA Modules:
  0.0 38.0 jit_solution(14572514703625195364)
XLA Ops:
  1.3 34.4 %shard_map.73 = (f32[5,2,16,256]{3,2,1,0:T(8,128)}, f32[5,1,256]{2,1,0:T(1,128)}) custom-call(s32[1]{0:T(128)S(6)} %copy.12.offsets, s32[1,1]{1,0:T(1,128)S(6)} %copy.11.sources, f32[5,2,16,256]{3,2,1,0:T(8,128)} %params.1, f32[1,1,9,8,16,256]{5,4,3,2,1,0:T(8,128)} %adjoint.1, bf16[1,1,6,3,8,16,256]{6,5,4,3,2,1,0:T(8,128)(2,1)} %snapshots.1, ...), custom_call_target="tpu_custom_call" | custom-call | tf_op jit(solution)/shard_map/pallas_call | solution.py:457
  35.7 0.7 %copy.10 = f32[5,1,256]{2,0,1:T(8,128)S(1)} copy(f32[5,1,256]{2,1,0:T(1,128)} %get-tuple-element.8) | data formatting | bytes 10240
  36.4 1.6 %broadcast_multiply_fusion = f32[5,2,16,256]{3,2,1,0:T(8,128)} fusion(f32[5,2,16,256]{3,2,1,0:T(8,128)} %get-tuple-element.7, f32[5,256]{1,0:T(8,128)S(1)} %bitcast.5), kind=kLoop, calls=%fused_computation | loop fusion | flops 40960 | bytes 332800 | tf_op jit(solution)/shard_map/mul | solution.py:496

commit v4 on v3

--- a/solution.py
+++ b/solution.py
@@ -64,43 +64,7 @@
     return at
 
 
-def kernel(
-    tiles,
-    offsets,
-    sources,
-    params,
-    adjoint,
-    snapshots,
-    residuals,
-    receivers,
-    summed,
-    scales,
-    out,
-    offset,
-    source_at,
-    window,
-    state,
-    snaps,
-    resid,
-    recs,
-    inject,
-    fields,
-    coef,
-    grad,
-    gwin,
-    fromp,
-    sumbuf,
-    landed,
-    mine,
-    maxima,
-    local_sem,
-    p_send,
-    p_recv,
-    g_send,
-    g_recv,
-    m_send,
-    m_recv,
-):
+def gather_kernel(tiles, params, window, p_send, p_recv, local_sem):
     me = lax.axis_index("tile")
     core = lax.rem(me, 2)
     xbit = lax.rem(lax.div(me, 2), 2)
@@ -109,28 +73,22 @@
     xn = me + 2 - 4 * xbit
     zf = me + 4 - 8 * xbit
     zr = me - 4 + 8 * xbit
-    nx = state.shape[1]
-    nf, slab = params.shape[:2]
-    ny, nz = state.shape[2], state.shape[3]
+    nf = params.shape[0]
+    own_copy = pltpu.make_async_copy(params, window.at[REACH], local_sem.at[0])
+    own_copy.start()
 
     barrier = pltpu.get_barrier_semaphore()
-
-    @pl.loop(1, tiles)
-    def _(d):
-        pl.semaphore_signal(
-            barrier, inc=1, device_id={"tile": lax.rem(me + d, tiles)}, device_id_type=MESH
-        )
-
-    own_copy = pltpu.make_async_copy(params, window.at[REACH], local_sem.at[0])
-    state_copy = pltpu.make_async_copy(adjoint.at[0, 0], state, local_sem.at[1])
-    snap_copy = pltpu.make_async_copy(snapshots.at[0, 0], snaps, local_sem.at[2])
-    resid_copy = pltpu.make_async_copy(residuals, resid, local_sem.at[3])
-    recs_copy = pltpu.make_async_copy(receivers, recs, local_sem.at[4])
-    offset_copy = pltpu.make_async_copy(offsets, offset, local_sem.at[5])
-    source_copy = pltpu.make_async_copy(sources, source_at, local_sem.at[6])
-    for copy in (recs_copy, resid_copy, snap_copy, own_copy, state_copy, offset_copy, source_copy):
-        copy.start()
-    pl.semaphore_wait(barrier, tiles - 1)
+    greeted = [partner, xn, zf, zr, far]
+    for t in greeted:
+
+        def greet(t=t):
+            pl.semaphore_signal(barrier, inc=1, device_id={"tile": t}, device_id_type=MESH)
+
+        pl.when(jnp.logical_and(t >= 0, t < tiles))(greet)
+    peers = 0
+    for t in greeted:
+        peers = peers + jnp.where(jnp.logical_and(t >= 0, t < tiles), 1, 0)
+    pl.semaphore_wait(barrier, peers)
 
     def push(src, dst, send, recv, to):
         return pltpu.make_async_remote_copy(
@@ -177,33 +135,61 @@
     def gone(block, sem):
         push(block, block, sem, p_recv.at[0], partner).wait_send()
 
-    recs_copy.wait()
-    resid_copy.wait()
-    snap_copy.wait()
+    def pass_z(f):
+        def go():
+            got(window.at[slot_z, f], p_recv.at[5 + f])
+            relay_z(f).start()
+
+        when_in(zr, go)
+
+    for f in range(nf):
+        got(window.at[slot_x, f], p_recv.at[f])
+        when_in(zf, on_z(f).start)
+        relay_x(f).start()
+        if f >= 2:
+            pass_z(f - 2)
+    pass_z(nf - 2)
+    pass_z(nf - 1)
+    got(window.at[4 - 2 * core], p_recv.at[10])
+    when_in(far, lambda: got(window.at[6 * core], p_recv.at[11]))
+    got(window.at[slot_x - to_core], p_recv.at[12])
+    when_in(zr, lambda: got(window.at[slot_z - to_core], p_recv.at[13]))
+    own_copy.wait()
+    gone(params, p_send.at[0])
+    send_own.wait_send()
+    when_in(far, send_far.wait_send)
+    when_in(zf, lambda: gone(window.at[slot_x], p_send.at[3]))
+    gone(window.at[slot_x], p_send.at[4])
+    when_in(zr, lambda: gone(window.at[slot_z], p_send.at[5]))
+
+
+def compute_kernel(
+    offsets,
+    sources,
+    window,
+    adjoint,
+    snaps,
+    resid,
+    recs,
+    gwin,
+    state,
+    inject,
+    fields,
+    coef,
+    grad,
+):
+    me = lax.axis_index("tile")
+    nx = state.shape[1]
+    nf, slab = window.shape[1:3]
+    ny, nz = state.shape[2], state.shape[3]
+    state[...] = adjoint[...]
     cells = recs[...]
     lanes = cells.shape[1]
     rows = nx * ny
     blocks = [(r, c) for r in range(ny // 8) for c in range(nz // 128)]
 
-    def pass_z(f):
-        def go():
-            got(window.at[slot_z, f], p_recv.at[5 + f])
-            relay_z(f).start()
-
-        when_in(zr, go)
-
     @pl.loop(0, STEPS)
     def _(s):
-        @pl.when(s < nf)
-        def _():
-            got(window.at[slot_x, s], p_recv.at[s])
-            when_in(zf, lambda: on_z(s).start())
-            relay_x(s).start()
-
-        @pl.when(s >= 2)
-        def _():
-            pass_z(s - 2)
-
         def velocity(i):
             planes = []
             for c in range(3):
@@ -250,17 +236,7 @@
         total = terms[:rows] + (terms[rows : 2 * rows] + terms[2 * rows :])
         inject[s] = total.reshape(nx, ny, nz)
 
-    pass_z(nf - 1)
-    got(window.at[4 - 2 * core], p_recv.at[10])
-    when_in(far, lambda: got(window.at[6 * core], p_recv.at[11]))
-    got(window.at[slot_x - to_core], p_recv.at[12])
-    when_in(zr, lambda: got(window.at[slot_z - to_core], p_recv.at[13]))
-    own_copy.wait()
-    state_copy.wait()
-
-    offset_copy.wait()
-    source_copy.wait()
-    rel = jnp.clip(offset[0] - me + REACH, 0, REACH)
+    rel = jnp.clip(offsets[0] - me + REACH, 0, REACH)
     for j in range(APER):
         b, c11, c13, c33, c44 = [window[rel + j, f] for f in range(5)]
         here = slice(j * slab, (j + 1) * slab)
@@ -334,7 +310,7 @@
                 velocity(i + 1)
             stress(i)
 
-    source = source_at[0, 0]
+    source = sources[0, 0]
     sx = lax.div(source, ny * nz)
     sy = lax.rem(lax.div(source, nz), ny)
     sz = lax.rem(source, nz)
@@ -360,18 +336,63 @@
             for k in range(slab):
                 gwin[pos, f, k] = jnp.where(ok, grad[f, start + k], 0.0)
 
+    for pos in range(SPAN):
+        place(pos)
+
+
+def reduce_kernel(
+    tiles, gwin, out, fromp, sumbuf, landed, mine, maxima, g_send, g_recv, m_send, m_recv
+):
+    me = lax.axis_index("tile")
+    core = lax.rem(me, 2)
+    xbit = lax.rem(lax.div(me, 2), 2)
+    partner = me + 1 - 2 * core
+    far = me + 3 * (2 * core - 1)
+    xn = me + 2 - 4 * xbit
+    zf = me + 4 - 8 * xbit
+    zr = me - 4 + 8 * xbit
+    nf = gwin.shape[1]
+
+    barrier = pltpu.get_barrier_semaphore()
+
+    @pl.loop(1, tiles)
+    def _(d):
+        pl.semaphore_signal(
+            barrier, inc=1, device_id={"tile": lax.rem(me + d, tiles)}, device_id_type=MESH
+        )
+
+    pl.semaphore_wait(barrier, tiles - 1)
+
+    def push(src, dst, send, recv, to):
+        return pltpu.make_async_remote_copy(
+            src_ref=src,
+            dst_ref=dst,
+            send_sem=send,
+            recv_sem=recv,
+            device_id={"tile": to},
+            device_id_type=MESH,
+        )
+
+    def when_in(t, fn):
+        pl.when(jnp.logical_and(t >= 0, t < tiles))(fn)
+
+    slot_x = 5 - 4 * xbit
+    slot_z = 1 + 4 * xbit
+    to_core = 2 * core - 1
+
+    def got(block, sem):
+        push(block, block, g_send.at[0], sem, partner).wait_recv()
+
+    def gone(block, sem):
+        push(block, block, sem, g_recv.at[0], partner).wait_send()
+
     pair = [
         push(gwin.at[pos - to_core], fromp.at[k], g_send.at[k], g_recv.at[10 + k], partner)
         for k, pos in enumerate((slot_z, slot_x, REACH))
     ]
     to_far = push(gwin.at[6 * core], landed.at[2], g_send.at[5], g_recv.at[13], far)
     for k, pos in enumerate((slot_z, slot_x, REACH)):
-        place(pos - to_core)
         pair[k].start()
-    place(slot_z)
-    place(6 * core)
-    place(slot_x)
-    place(REACH)
 
     def to_z(f):
         return push(sumbuf.at[0, f], landed.at[0, f], g_send.at[3], g_recv.at[5 + f], zr)
@@ -421,28 +442,16 @@
     def _(d):
         max_copy(d).start()
 
-    store = pltpu.make_async_copy(out, summed, local_sem.at[7])
-    store.start()
-
-    gone(params, p_send.at[0])
-    send_own.wait_send()
-    when_in(far, send_far.wait_send)
-    when_in(zf, lambda: gone(window.at[slot_x], p_send.at[3]))
-    gone(window.at[slot_x], p_send.at[4])
-    when_in(zr, lambda: gone(window.at[slot_z], p_send.at[5]))
     for copy in pair:
         copy.wait_send()
     when_in(far, to_far.wait_send)
     when_in(zr, lambda: gone(sumbuf.at[0], g_send.at[3]))
     gone(sumbuf.at[1], g_send.at[4])
-
     got(maxima, m_recv.at[0])
     scale = 1.0 / (jnp.maximum(jnp.max(maxima[...], axis=0), row) + EPSILON)
     for f in range(nf):
-        factor = jnp.sum(jnp.where(lane == f, scale, 0.0), axis=1, keepdims=True)
-        scales[f] = jnp.broadcast_to(factor, (1, nz))
+        out[f] = out[f] * jnp.sum(jnp.where(lane == f, scale, 0.0), axis=1, keepdims=True)
     gone(maxima, m_send.at[0])
-    store.wait()
 
 
 def on_device(params, adjoint_state, snapshots, residuals, receivers, sources, offsets):
@@ -450,50 +459,56 @@
     grid = adjoint_state.shape[3:]
     slab_shape = params.shape
     f32 = jnp.float32
-    hbm = pl.BlockSpec(memory_space=pltpu.HBM)
+    hbm = pl.BlockSpec(memory_space=pl.ANY)
+    smem = pl.BlockSpec(memory_space=pltpu.SMEM)
     vmem = pl.BlockSpec(memory_space=pltpu.VMEM)
     dma = pltpu.SemaphoreType.DMA
+    mib = 1024 * 1024
     rows = jnp.transpose(residuals[0], (1, 0, 2))
-    summed, scales = pl.pallas_call(
-        functools.partial(kernel, tiles),
-        out_shape=[
-            jax.ShapeDtypeStruct(slab_shape, f32),
-            jax.ShapeDtypeStruct((slab_shape[0], 1, slab_shape[3]), f32),
-        ],
-        in_specs=[hbm, hbm, hbm, hbm, hbm, hbm, hbm],
-        out_specs=[hbm, vmem],
+    window = pl.pallas_call(
+        functools.partial(gather_kernel, tiles),
+        out_shape=jax.ShapeDtypeStruct((SPAN,) + slab_shape, f32),
+        in_specs=[hbm],
+        out_specs=vmem,
+        scratch_shapes=[dma((6,)), dma((14,)), dma((1,))],
+        compiler_params=pltpu.CompilerParams(
+            collective_id=0, has_side_effects=True, vmem_limit_bytes=16 * mib
+        ),
+    )(params)
+    gwin = pl.pallas_call(
+        compute_kernel,
+        out_shape=jax.ShapeDtypeStruct((SPAN,) + slab_shape, f32),
+        in_specs=[smem, smem, vmem, vmem, vmem, vmem, vmem],
+        out_specs=vmem,
         scratch_shapes=[
-            pltpu.VMEM(slab_shape, f32),
-            pltpu.SMEM(offsets.shape, jnp.int32),
-            pltpu.SMEM(sources.shape, jnp.int32),
-            pltpu.VMEM((SPAN,) + slab_shape, f32),
             pltpu.VMEM((9,) + grid, f32),
-            pltpu.VMEM((STEPS, 3) + grid, jnp.bfloat16),
-            pltpu.VMEM(rows.shape, f32),
-            pltpu.VMEM(receivers.shape[1:], jnp.int32),
             pltpu.VMEM((STEPS,) + grid, f32),
             pltpu.VMEM((STEPS, 10) + grid, f32),
             pltpu.VMEM((6,) + grid, f32),
             pltpu.VMEM((5,) + grid, f32),
-            pltpu.VMEM((SPAN,) + slab_shape, f32),
+        ],
+        compiler_params=pltpu.CompilerParams(vmem_limit_bytes=32 * mib),
+    )(offsets, sources, window, adjoint_state[0, 0], snapshots[0, 0], rows, receivers[0])
+    return pl.pallas_call(
+        functools.partial(reduce_kernel, tiles),
+        out_shape=jax.ShapeDtypeStruct(slab_shape, f32),
+        in_specs=[vmem],
+        out_specs=vmem,
+        scratch_shapes=[
             pltpu.VMEM((3,) + slab_shape, f32),
             pltpu.VMEM((2,) + slab_shape, f32),
             pltpu.VMEM((3,) + slab_shape, f32),
             pltpu.VMEM((1, 128), f32),
             pltpu.VMEM((tiles - 1, 1, 128), f32),
-            dma((8,)),
-            dma((6,)),
-            dma((14,)),
             dma((6,)),
             dma((14,)),
             dma((1,)),
             dma((1,)),
         ],
         compiler_params=pltpu.CompilerParams(
-            collective_id=0, has_side_effects=True, vmem_limit_bytes=56 * 1024 * 1024
+            collective_id=1, has_side_effects=True, vmem_limit_bytes=16 * mib
         ),
-    )(offsets, sources, params, adjoint_state, snapshots, rows, receivers[0])
-    return summed * scales[:, :, None, :]
+    )(gwin)
 
 
 def solution(mesh):

time: 38.2 us -> 40.7 us (1.065)
  local copies, waits for them, and re-layouts: 0.69 us -> 2.85 us
  Pallas kernels: 34.4 us -> 36.2 us
  other arithmetic: 1.6 us -> 0 us
    unnamed x1 -> x11, local copies, waits for them, and re-layouts: 0.69 us -> 2.85 us
    pallas_call x1 -> x3, Pallas kernels: 34.4 us -> 36.2 us  [the longest x1 20.5 us: on_device(): pl.pallas_call(functools.partial(reduce_kernel, tiles), out_shape=jax.Sha...]
    mul x1 -> x0, other arithmetic: 1.6 us -> none  [on_device(): return summed * scales[:, :, None, :]]
where the time goes in v4:
time: 40.7 us; the launch traced here: 40.5 us
  Pallas kernels  36.2 us (89%)
  local copies, waits for them, and re-layouts  2.85 us (7%)
  between operations  1.46 us (4%)
    pallas_call x1, Pallas kernels, on_device(): pl.pallas_call(functools.partial(reduce_kernel, tiles), out_shape=jax.Sha...  20.5 us
    pallas_call x1, Pallas kernels, on_device(): pl.pallas_call(functools.partial(gather_kernel, tiles), out_shape=jax.Sha...  11.1 us
    pallas_call x1, Pallas kernels, on_device(): pl.pallas_call(compute_kernel, out_shape=jax.ShapeDtypeStruct((SPAN,) + s...  4.65 us
    unnamed x11, local copies, waits for them, and re-layouts  2.85 us

profile of v4, /device:TPU:0, one launch (start us, length us, event | category | flops | bytes accessed | tf_op | source)
XLA Modules:
  0.0 40.5 jit_solution(17790472935110705174)
XLA Ops:
  0.0 0.0 copy-start
  1.4 0.0 copy-start.2
  1.4 0.9 %copy-done.2 = f32[5,2,16,256]{3,2,1,0:T(8,128)S(1)} copy-done((f32[5,2,16,256]{3,2,1,0:T(8,128)S(1)}, f32[5,2,16,256]{3,2,1,0:T(8,128)}, u32[]{:S(2)}) %copy-start.2) | copy-done | bytes 163864
  2.3 0.0 copy-start.3
  2.3 0.0 copy-start.4
  2.3 11.1 %shard_map.73.window = f32[7,5,2,16,256]{4,3,2,1,0:T(8,128)S(1)} custom-call(f32[5,2,16,256]{3,2,1,0:T(8,128)S(1)} %copy-done.2), custom_call_target="tpu_custom_call" | custom-call | tf_op jit(solution)/shard_map/pallas_call | solution.py:468
  13.4 0.0 copy-done
  13.4 0.0 copy-done.3
  13.4 0.0 copy-done.4
  13.4 0.0 copy-start.1
  13.4 1.3 %copy-done.1 = bf16[1,1,6,3,8,16,256]{6,5,4,3,2,1,0:T(8,128)(2,1)S(1)} copy-done((bf16[1,1,6,3,8,16,256]{6,5,4,3,2,1,0:T(8,128)(2,1)S(1)}, bf16[1,1,6,3,8,16,256]{6,5,4,3,2,1,0:T(8,128)(2,1)}, u32[]{:S(2)}) %copy-start.1) | copy-done | bytes 1179672
  14.7 4.7 %shard_map.74.gwin = f32[7,5,2,16,256]{4,3,2,1,0:T(8,128)S(1)} custom-call(s32[1]{0:T(128)S(6)} %copy.10.offsets, s32[1,1]{1,0:T(1,128)S(6)} %copy.9.sources, f32[7,5,2,16,256]{4,3,2,1,0:T(8,128)S(1)} %shard_map.73.window, f32[9,8,16,256]{3,2,1,0:T(8,128)S(1)} %bitcast.4, bf16[6,3,8,16,256]{4,3,2,1,0:T(8,128)(2,1)S(1)} %bitcast.5, f32[6,1,256]{2,1,0:T(1,128)S(1)} %bitcast.6, ...), custom_call_target="tpu_custom_call" | custom-call | tf_op jit(solution)/shard_map/pallas_call | solution.py:478
  19.3 20.5 %shard_map.75 = f32[5,2,16,256]{3,2,1,0:T(8,128)S(1)} custom-call(f32[7,5,2,16,256]{4,3,2,1,0:T(8,128)S(1)} %shard_map.74.gwin), custom_call_target="tpu_custom_call" | custom-call | tf_op jit(solution)/shard_map/pallas_call | solution.py:492
  39.8 0.7 %copy.11 = f32[5,2,16,256]{3,2,1,0:T(8,128)} copy(f32[5,2,16,256]{3,2,1,0:T(8,128)S(1)} %shard_map.75) | data formatting | bytes 327680
Async XLA Ops:
  0.0 13.4 %copy-start = (f32[1,1,9,8,16,256]{5,4,3,2,1,0:T(8,128)S(1)}, f32[1,1,9,8,16,256]{5,4,3,2,1,0:T(8,128)}, u32[]{:S(2)}) copy-start(f32[1,1,9,8,16,256]{5,4,3,2,1,0:T(8,128)} %param.8) | copy-start | bytes 3538948
  1.4 0.9 %copy-start.2 = (f32[5,2,16,256]{3,2,1,0:T(8,128)S(1)}, f32[5,2,16,256]{3,2,1,0:T(8,128)}, u32[]{:S(2)}) copy-start(f32[5,2,16,256]{3,2,1,0:T(8,128)} %params.1) | copy-start | bytes 491524
  2.3 11.1 %copy-start.3 = (f32[1,1,6,256]{3,1,2,0:T(1,128)S(1)}, f32[1,1,6,256]{3,1,2,0:T(1,128)}, u32[]{:S(2)}) copy-start(f32[1,1,6,256]{3,1,2,0:T(1,128)} %param.10) | copy-start | bytes 18436
  2.3 11.1 %copy-start.4 = (s32[1,1,256]{2,1,0:T(1,128)S(1)}, s32[1,1,256]{2,1,0:T(1,128)}, u32[]{:S(2)}) copy-start(s32[1,1,256]{2,1,0:T(1,128)} %param.11) | copy-start | bytes 3076
  13.4 1.3 %copy-start.1 = (bf16[1,1,6,3,8,16,256]{6,5,4,3,2,1,0:T(8,128)(2,1)S(1)}, bf16[1,1,6,3,8,16,256]{6,5,4,3,2,1,0:T(8,128)(2,1)}, u32[]{:S(2)}) copy-start(bf16[1,1,6,3,8,16,256]{6,5,4,3,2,1,0:T(8,128)(2,1)} %param.9) | copy-start | bytes 3538948

commit v5 on v3

--- a/solution.py
+++ b/solution.py
@@ -73,8 +73,6 @@
     snapshots,
     residuals,
     receivers,
-    summed,
-    scales,
     out,
     offset,
     source_at,
@@ -360,32 +358,46 @@
             for k in range(slab):
                 gwin[pos, f, k] = jnp.where(ok, grad[f, start + k], 0.0)
 
-    pair = [
-        push(gwin.at[pos - to_core], fromp.at[k], g_send.at[k], g_recv.at[10 + k], partner)
-        for k, pos in enumerate((slot_z, slot_x, REACH))
-    ]
-    to_far = push(gwin.at[6 * core], landed.at[2], g_send.at[5], g_recv.at[13], far)
-    for k, pos in enumerate((slot_z, slot_x, REACH)):
-        place(pos - to_core)
-        pair[k].start()
+    def pair_z(f):
+        block = gwin.at[slot_z - to_core, f]
+        return push(block, fromp.at[0, f], g_send.at[0], g_recv.at[10 + f], partner)
+
+    def pair_x(f):
+        block = gwin.at[slot_x - to_core, f]
+        return push(block, fromp.at[1, f], g_send.at[1], g_recv.at[15 + f], partner)
+
+    pair_own = push(gwin.at[REACH - to_core], fromp.at[2], g_send.at[2], g_recv.at[20], partner)
+
+    def to_far(f):
+        return push(gwin.at[6 * core, f], landed.at[2, f], g_send.at[5], g_recv.at[21], far)
+
+    def to_z(f):
+        return push(sumbuf.at[0, f], landed.at[0, f], g_send.at[3], g_recv.at[5 + f], zr)
+
+    def to_x(f):
+        return push(sumbuf.at[1, f], landed.at[1, f], g_send.at[4], g_recv.at[f], xn)
+
+    place(slot_z - to_core)
+    for f in range(nf):
+        pair_z(f).start()
+    place(6 * core)
+    when_in(far, to_far(0).start)
+    place(slot_x - to_core)
+    for f in range(nf):
+        pair_x(f).start()
     place(slot_z)
-    place(6 * core)
+    for f in range(nf):
+        pair_z(f).wait_recv()
+        sumbuf[0, f] = gwin[slot_z, f] + fromp[0, f]
+        when_in(zr, to_z(f).start)
+    for f in range(1, nf):
+        when_in(far, to_far(f).start)
+    place(REACH - to_core)
+    pair_own.start()
     place(slot_x)
     place(REACH)
-
-    def to_z(f):
-        return push(sumbuf.at[0, f], landed.at[0, f], g_send.at[3], g_recv.at[5 + f], zr)
-
-    def to_x(f):
-        return push(sumbuf.at[1, f], landed.at[1, f], g_send.at[4], g_recv.at[f], xn)
-
-    pair[0].wait_recv()
-    for f in range(nf):
-        sumbuf[0, f] = gwin[slot_z, f] + fromp[0, f]
-        when_in(zr, to_z(f).start)
-    when_in(far, to_far.start)
-    pair[1].wait_recv()
-    for f in range(nf):
+    for f in range(nf):
+        pair_x(f).wait_recv()
         sumbuf[1, f] = gwin[slot_x, f] + fromp[1, f]
 
         def join(f=f):
@@ -394,11 +406,11 @@
 
         when_in(zf, join)
         to_x(f).start()
-    pair[2].wait_recv()
+    pair_own.wait_recv()
     out[...] = gwin[REACH] + fromp[2]
 
     def join_far():
-        got(landed.at[2], g_recv.at[13])
+        got(landed.at[2], g_recv.at[21])
         out[...] += landed[2]
 
     when_in(far, join_far)
@@ -421,28 +433,24 @@
     def _(d):
         max_copy(d).start()
 
-    store = pltpu.make_async_copy(out, summed, local_sem.at[7])
-    store.start()
-
     gone(params, p_send.at[0])
     send_own.wait_send()
     when_in(far, send_far.wait_send)
     when_in(zf, lambda: gone(window.at[slot_x], p_send.at[3]))
     gone(window.at[slot_x], p_send.at[4])
     when_in(zr, lambda: gone(window.at[slot_z], p_send.at[5]))
-    for copy in pair:
-        copy.wait_send()
-    when_in(far, to_far.wait_send)
+    gone(fromp.at[0], g_send.at[0])
+    gone(fromp.at[1], g_send.at[1])
+    pair_own.wait_send()
+    when_in(far, lambda: gone(landed.at[2], g_send.at[5]))
     when_in(zr, lambda: gone(sumbuf.at[0], g_send.at[3]))
     gone(sumbuf.at[1], g_send.at[4])
 
     got(maxima, m_recv.at[0])
     scale = 1.0 / (jnp.maximum(jnp.max(maxima[...], axis=0), row) + EPSILON)
     for f in range(nf):
-        factor = jnp.sum(jnp.where(lane == f, scale, 0.0), axis=1, keepdims=True)
-        scales[f] = jnp.broadcast_to(factor, (1, nz))
+        out[f] = out[f] * jnp.sum(jnp.where(lane == f, scale, 0.0), axis=1, keepdims=True)
     gone(maxima, m_send.at[0])
-    store.wait()
 
 
 def on_device(params, adjoint_state, snapshots, residuals, receivers, sources, offsets):
@@ -454,16 +462,12 @@
     vmem = pl.BlockSpec(memory_space=pltpu.VMEM)
     dma = pltpu.SemaphoreType.DMA
     rows = jnp.transpose(residuals[0], (1, 0, 2))
-    summed, scales = pl.pallas_call(
+    return pl.pallas_call(
         functools.partial(kernel, tiles),
-        out_shape=[
-            jax.ShapeDtypeStruct(slab_shape, f32),
-            jax.ShapeDtypeStruct((slab_shape[0], 1, slab_shape[3]), f32),
-        ],
+        out_shape=jax.ShapeDtypeStruct(slab_shape, f32),
         in_specs=[hbm, hbm, hbm, hbm, hbm, hbm, hbm],
-        out_specs=[hbm, vmem],
+        out_specs=vmem,
         scratch_shapes=[
-            pltpu.VMEM(slab_shape, f32),
             pltpu.SMEM(offsets.shape, jnp.int32),
             pltpu.SMEM(sources.shape, jnp.int32),
             pltpu.VMEM((SPAN,) + slab_shape, f32),
@@ -485,7 +489,7 @@
             dma((6,)),
             dma((14,)),
             dma((6,)),
-            dma((14,)),
+            dma((22,)),
             dma((1,)),
             dma((1,)),
         ],
@@ -493,7 +497,6 @@
             collective_id=0, has_side_effects=True, vmem_limit_bytes=56 * 1024 * 1024
         ),
     )(offsets, sources, params, adjoint_state, snapshots, rows, receivers[0])
-    return summed * scales[:, :, None, :]
 
 
 def solution(mesh):

time: 38.2 us -> 37.4 us (0.979)
  other arithmetic: 1.6 us -> 0 us
  local copies, waits for them, and re-layouts: 0.69 us -> 1.59 us
    mul x1 -> x0, other arithmetic: 1.6 us -> none  [on_device(): return summed * scales[:, :, None, :]]
    unnamed x1, local copies, waits for them, and re-layouts: 0.69 us -> 1.59 us
where the time goes in v5:
time: 37.4 us; the launch traced here: 37.2 us
  Pallas kernels  34.3 us (92%)
  local copies, waits for them, and re-layouts  1.59 us (4%)
  between operations  1.3 us (3%)
    pallas_call x1, Pallas kernels, on_device(): pl.pallas_call(functools.partial(kernel, tiles), out_shape=jax.ShapeDtype...  34.3 us
    unnamed x1, local copies, waits for them, and re-layouts  1.59 us

profile of v5, /device:TPU:0, one launch (start us, length us, event | category | flops | bytes accessed | tf_op | source)
XLA Modules:
  0.0 37.2 jit_solution(2649396196800099972)
XLA Ops:
  1.3 34.3 %shard_map.73 = f32[5,2,16,256]{3,2,1,0:T(8,128)} custom-call(s32[1]{0:T(128)S(6)} %copy.10.offsets, s32[1,1]{1,0:T(1,128)S(6)} %copy.9.sources, f32[5,2,16,256]{3,2,1,0:T(8,128)} %params.1, f32[1,1,9,8,16,256]{5,4,3,2,1,0:T(8,128)} %adjoint.1, bf16[1,1,6,3,8,16,256]{6,5,4,3,2,1,0:T(8,128)(2,1)} %snapshots.1, f32[6,1,256]{2,1,0:T(1,128)} %bitcast.2, ...), custom_call_target="tpu_custom_call" | custom-call | tf_op jit(solution)/shard_map/pallas_call | solution.py:465
  35.6 1.6 %copy.11 = f32[5,2,16,256]{3,2,1,0:T(8,128)} copy(f32[5,2,16,256]{3,2,1,0:T(8,128)} %shard_map.73) | data formatting | bytes 327680

commit v6 on v5

--- a/solution.py
+++ b/solution.py
@@ -107,6 +107,7 @@
     xn = me + 2 - 4 * xbit
     zf = me + 4 - 8 * xbit
     zr = me - 4 + 8 * xbit
+    dg = me - 2 + 4 * xbit
     nx = state.shape[1]
     nf, slab = params.shape[:2]
     ny, nz = state.shape[2], state.shape[3]
@@ -147,27 +148,38 @@
     slot_z = 1 + 4 * xbit
     to_core = 2 * core - 1
 
-    def send_x(f):
-        return push(params.at[f], window.at[slot_z, f], p_send.at[0], p_recv.at[f], xn)
+    chunks = [pl.ds(0, 1), pl.ds(1, 2), pl.ds(3, 2)]
+    passed = pl.ds(0, 3)
+
+    def send_x(k):
+        block = window.at[slot_z, chunks[k]]
+        return push(params.at[chunks[k]], block, p_send.at[0], p_recv.at[k], xn)
 
     send_own = push(params, window.at[2 + 2 * core], p_send.at[1], p_recv.at[10], partner)
     send_far = push(params, window.at[6 - 6 * core], p_send.at[2], p_recv.at[11], far)
-    for f in range(nf):
-        send_x(f).start()
+    send_dg = push(
+        params.at[chunks[2]], window.at[slot_x, chunks[2]], p_send.at[6], p_recv.at[5], dg
+    )
+    send_x(0).start()
+    send_x(1).start()
+    when_in(far, send_far.start)
+    when_in(dg, send_dg.start)
+    send_x(2).start()
     send_own.start()
-    when_in(far, send_far.start)
-
-    def on_z(f):
-        block = window.at[slot_x, f]
-        return push(block, window.at[slot_z, f], p_send.at[3], p_recv.at[5 + f], zf)
-
-    def relay_x(f):
-        block = window.at[slot_x, f]
-        return push(block, window.at[slot_x + to_core, f], p_send.at[4], p_recv.at[12], partner)
-
-    def relay_z(f):
-        block = window.at[slot_z, f]
-        return push(block, window.at[slot_z + to_core, f], p_send.at[5], p_recv.at[13], partner)
+
+    def on_z(k):
+        block = window.at[slot_x, chunks[k]]
+        return push(block, window.at[slot_z, chunks[k]], p_send.at[3], p_recv.at[3 + k], zf)
+
+    def relay_x(k):
+        block = window.at[slot_x, chunks[k]]
+        there = window.at[slot_x + to_core, chunks[k]]
+        return push(block, there, p_send.at[4], p_recv.at[12], partner)
+
+    def relay_z(k):
+        block = window.at[slot_z, chunks[k]]
+        there = window.at[slot_z + to_core, chunks[k]]
+        return push(block, there, p_send.at[5], p_recv.at[13], partner)
 
     def got(block, sem):
         push(block, block, p_send.at[0], sem, partner).wait_recv()
@@ -183,24 +195,25 @@
     rows = nx * ny
     blocks = [(r, c) for r in range(ny // 8) for c in range(nz // 128)]
 
-    def pass_z(f):
-        def go():
-            got(window.at[slot_z, f], p_recv.at[5 + f])
-            relay_z(f).start()
-
-        when_in(zr, go)
+    def pass_x(k):
+        got(window.at[slot_x, chunks[k]], p_recv.at[k])
+        if k < 2:
+            when_in(zf, on_z(k).start)
+        relay_x(k).start()
+
+    def pass_z(k):
+        got(window.at[slot_z, chunks[k]], p_recv.at[3 + k])
+        relay_z(k).start()
 
     @pl.loop(0, STEPS)
     def _(s):
-        @pl.when(s < nf)
+        @pl.when(s == 3)
         def _():
-            got(window.at[slot_x, s], p_recv.at[s])
-            when_in(zf, lambda: on_z(s).start())
-            relay_x(s).start()
-
-        @pl.when(s >= 2)
+            pass_x(0)
+
+        @pl.when(s == 5)
         def _():
-            pass_z(s - 2)
+            pass_x(1)
 
         def velocity(i):
             planes = []
@@ -248,7 +261,9 @@
         total = terms[:rows] + (terms[rows : 2 * rows] + terms[2 * rows :])
         inject[s] = total.reshape(nx, ny, nz)
 
-    pass_z(nf - 1)
+    pass_x(2)
+    for k in range(3):
+        when_in(zr, functools.partial(pass_z, k))
     got(window.at[4 - 2 * core], p_recv.at[10])
     when_in(far, lambda: got(window.at[6 * core], p_recv.at[11]))
     got(window.at[slot_x - to_core], p_recv.at[12])
@@ -358,54 +373,54 @@
             for k in range(slab):
                 gwin[pos, f, k] = jnp.where(ok, grad[f, start + k], 0.0)
 
-    def pair_z(f):
-        block = gwin.at[slot_z - to_core, f]
-        return push(block, fromp.at[0, f], g_send.at[0], g_recv.at[10 + f], partner)
-
-    def pair_x(f):
-        block = gwin.at[slot_x - to_core, f]
-        return push(block, fromp.at[1, f], g_send.at[1], g_recv.at[15 + f], partner)
-
+    def pair_z(k):
+        block = gwin.at[slot_z - to_core, chunks[k]]
+        return push(block, fromp.at[0, chunks[k]], g_send.at[0], g_recv.at[10 + k], partner)
+
+    pair_x = push(gwin.at[slot_x - to_core], fromp.at[1], g_send.at[1], g_recv.at[13], partner)
     pair_own = push(gwin.at[REACH - to_core], fromp.at[2], g_send.at[2], g_recv.at[20], partner)
-
-    def to_far(f):
-        return push(gwin.at[6 * core, f], landed.at[2, f], g_send.at[5], g_recv.at[21], far)
-
-    def to_z(f):
-        return push(sumbuf.at[0, f], landed.at[0, f], g_send.at[3], g_recv.at[5 + f], zr)
-
-    def to_x(f):
-        return push(sumbuf.at[1, f], landed.at[1, f], g_send.at[4], g_recv.at[f], xn)
+    to_far = push(gwin.at[6 * core], landed.at[2], g_send.at[5], g_recv.at[21], far)
+
+    def to_z(k):
+        block = sumbuf.at[0, chunks[k]]
+        return push(block, landed.at[0, chunks[k]], g_send.at[3], g_recv.at[3 + k], zr)
+
+    to_dg = push(
+        sumbuf.at[0, chunks[2]], landed.at[0, chunks[2]], g_send.at[6], g_recv.at[5], dg
+    )
+
+    def to_x(k):
+        block = sumbuf.at[1, chunks[k]]
+        return push(block, landed.at[1, chunks[k]], g_send.at[4], g_recv.at[k], xn)
 
     place(slot_z - to_core)
-    for f in range(nf):
-        pair_z(f).start()
+    for k in range(3):
+        pair_z(k).start()
+    place(slot_x - to_core)
+    pair_x.start()
+    place(slot_z)
     place(6 * core)
-    when_in(far, to_far(0).start)
-    place(slot_x - to_core)
-    for f in range(nf):
-        pair_x(f).start()
-    place(slot_z)
-    for f in range(nf):
-        pair_z(f).wait_recv()
-        sumbuf[0, f] = gwin[slot_z, f] + fromp[0, f]
-        when_in(zr, to_z(f).start)
-    for f in range(1, nf):
-        when_in(far, to_far(f).start)
+    for k in range(3):
+        pair_z(k).wait_recv()
+        sumbuf[0, chunks[k]] = gwin[slot_z, chunks[k]] + fromp[0, chunks[k]]
+        when_in(zr, to_z(k).start if k < 2 else to_dg.start)
+        if k == 1:
+            when_in(far, to_far.start)
     place(REACH - to_core)
     pair_own.start()
     place(slot_x)
     place(REACH)
-    for f in range(nf):
-        pair_x(f).wait_recv()
-        sumbuf[1, f] = gwin[slot_x, f] + fromp[1, f]
-
-        def join(f=f):
-            got(landed.at[0, f], g_recv.at[5 + f])
-            sumbuf[1, f] += landed[0, f]
+    pair_x.wait_recv()
+    sumbuf[1] = gwin[slot_x] + fromp[1]
+    to_x(2).start()
+    for k in range(2):
+
+        def join(k=k):
+            got(landed.at[0, chunks[k]], g_recv.at[3 + k])
+            sumbuf[1, chunks[k]] += landed[0, chunks[k]]
 
         when_in(zf, join)
-        to_x(f).start()
+        to_x(k).start()
     pair_own.wait_recv()
     out[...] = gwin[REACH] + fromp[2]
 
@@ -413,12 +428,18 @@
         got(landed.at[2], g_recv.at[21])
         out[...] += landed[2]
 
+    def join_dg():
+        got(landed.at[0, chunks[2]], g_recv.at[5])
+        out[chunks[2]] += landed[0, chunks[2]]
+
     when_in(far, join_far)
+    when_in(zr, join_dg)
+    for k in (2, 0, 1):
+        got(landed.at[1, chunks[k]], g_recv.at[k])
 
     lane = lax.broadcasted_iota(jnp.int32, (1, 128), 1)
     row = jnp.zeros((1, 128), jnp.float32)
     for f in range(nf):
-        got(landed.at[1, f], g_recv.at[f])
         total = out[f] + landed[1, f]
         out[f] = total
         biggest = jnp.max(jnp.abs(total), axis=(0, 1, 2), keepdims=True)[0]
@@ -436,14 +457,16 @@
     gone(params, p_send.at[0])
     send_own.wait_send()
     when_in(far, send_far.wait_send)
-    when_in(zf, lambda: gone(window.at[slot_x], p_send.at[3]))
+    when_in(zf, lambda: gone(window.at[slot_x, passed], p_send.at[3]))
     gone(window.at[slot_x], p_send.at[4])
     when_in(zr, lambda: gone(window.at[slot_z], p_send.at[5]))
     gone(fromp.at[0], g_send.at[0])
-    gone(fromp.at[1], g_send.at[1])
+    pair_x.wait_send()
     pair_own.wait_send()
-    when_in(far, lambda: gone(landed.at[2], g_send.at[5]))
-    when_in(zr, lambda: gone(sumbuf.at[0], g_send.at[3]))
+    when_in(far, to_far.wait_send)
+    when_in(zr, lambda: gone(sumbuf.at[0, passed], g_send.at[3]))
+    when_in(zr, to_dg.wait_send)
+    when_in(dg, send_dg.wait_send)
     gone(sumbuf.at[1], g_send.at[4])
 
     got(maxima, m_recv.at[0])
@@ -486,9 +509,9 @@
             pltpu.VMEM((1, 128), f32),
             pltpu.VMEM((tiles - 1, 1, 128), f32),
             dma((8,)),
-            dma((6,)),
+            dma((7,)),
             dma((14,)),
-            dma((6,)),
+            dma((7,)),
             dma((22,)),
             dma((1,)),
             dma((1,)),

time: 37.4 us -> 35.7 us (0.955)
  Pallas kernels: 34.3 us -> 32.6 us
    pallas_call x1, Pallas kernels: 34.3 us -> 32.6 us  [on_device(): pl.pallas_call(functools.partial(kernel, tiles), out_shape=jax.ShapeDtype...]
where the time goes in v6:
time: 35.7 us; the launch traced here: 35.5 us
  Pallas kernels  32.6 us (91%)
  local copies, waits for them, and re-layouts  1.59 us (4%)
  between operations  1.3 us (4%)
    pallas_call x1, Pallas kernels, on_device(): pl.pallas_call(functools.partial(kernel, tiles), out_shape=jax.ShapeDtype...  32.6 us
    unnamed x1, local copies, waits for them, and re-layouts  1.59 us

profile of v6, /device:TPU:0, one launch (start us, length us, event | category | flops | bytes accessed | tf_op | source)
XLA Modules:
  0.0 35.5 jit_solution(9542693591503909357)
XLA Ops:
  1.3 32.6 %shard_map.73 = f32[5,2,16,256]{3,2,1,0:T(8,128)} custom-call(s32[1]{0:T(128)S(6)} %copy.10.offsets, s32[1,1]{1,0:T(1,128)S(6)} %copy.9.sources, f32[5,2,16,256]{3,2,1,0:T(8,128)} %params.1, f32[1,1,9,8,16,256]{5,4,3,2,1,0:T(8,128)} %adjoint.1, bf16[1,1,6,3,8,16,256]{6,5,4,3,2,1,0:T(8,128)(2,1)} %snapshots.1, f32[6,1,256]{2,1,0:T(1,128)} %bitcast.2, ...), custom_call_target="tpu_custom_call" | custom-call | tf_op jit(solution)/shard_map/pallas_call | solution.py:488
  33.9 1.6 %copy.11 = f32[5,2,16,256]{3,2,1,0:T(8,128)} copy(f32[5,2,16,256]{3,2,1,0:T(8,128)} %shard_map.73) | data formatting | bytes 327680

commit v7 on v6

--- a/solution.py
+++ b/solution.py
@@ -148,8 +148,8 @@
     slot_z = 1 + 4 * xbit
     to_core = 2 * core - 1
 
-    chunks = [pl.ds(0, 1), pl.ds(1, 2), pl.ds(3, 2)]
-    passed = pl.ds(0, 3)
+    chunks = [pl.ds(0, 2), pl.ds(2, 3)]
+    passed = pl.ds(0, 2)
 
     def send_x(k):
         block = window.at[slot_z, chunks[k]]
@@ -158,13 +158,12 @@
     send_own = push(params, window.at[2 + 2 * core], p_send.at[1], p_recv.at[10], partner)
     send_far = push(params, window.at[6 - 6 * core], p_send.at[2], p_recv.at[11], far)
     send_dg = push(
-        params.at[chunks[2]], window.at[slot_x, chunks[2]], p_send.at[6], p_recv.at[5], dg
+        params.at[chunks[1]], window.at[slot_x, chunks[1]], p_send.at[6], p_recv.at[4], dg
     )
     send_x(0).start()
-    send_x(1).start()
     when_in(far, send_far.start)
     when_in(dg, send_dg.start)
-    send_x(2).start()
+    send_x(1).start()
     send_own.start()
 
     def on_z(k):
@@ -197,7 +196,7 @@
 
     def pass_x(k):
         got(window.at[slot_x, chunks[k]], p_recv.at[k])
-        if k < 2:
+        if k == 0:
             when_in(zf, on_z(k).start)
         relay_x(k).start()
 
@@ -210,10 +209,6 @@
         @pl.when(s == 3)
         def _():
             pass_x(0)
-
-        @pl.when(s == 5)
-        def _():
-            pass_x(1)
 
         def velocity(i):
             planes = []
@@ -261,8 +256,8 @@
         total = terms[:rows] + (terms[rows : 2 * rows] + terms[2 * rows :])
         inject[s] = total.reshape(nx, ny, nz)
 
-    pass_x(2)
-    for k in range(3):
+    pass_x(1)
+    for k in range(2):
         when_in(zr, functools.partial(pass_z, k))
     got(window.at[4 - 2 * core], p_recv.at[10])
     when_in(far, lambda: got(window.at[6 * core], p_recv.at[11]))
@@ -386,7 +381,7 @@
         return push(block, landed.at[0, chunks[k]], g_send.at[3], g_recv.at[3 + k], zr)
 
     to_dg = push(
-        sumbuf.at[0, chunks[2]], landed.at[0, chunks[2]], g_send.at[6], g_recv.at[5], dg
+        sumbuf.at[0, chunks[1]], landed.at[0, chunks[1]], g_send.at[6], g_recv.at[4], dg
     )
 
     def to_x(k):
@@ -394,17 +389,17 @@
         return push(block, landed.at[1, chunks[k]], g_send.at[4], g_recv.at[k], xn)
 
     place(slot_z - to_core)
-    for k in range(3):
+    for k in range(2):
         pair_z(k).start()
     place(slot_x - to_core)
     pair_x.start()
     place(slot_z)
     place(6 * core)
-    for k in range(3):
+    for k in range(2):
         pair_z(k).wait_recv()
         sumbuf[0, chunks[k]] = gwin[slot_z, chunks[k]] + fromp[0, chunks[k]]
-        when_in(zr, to_z(k).start if k < 2 else to_dg.start)
-        if k == 1:
+        when_in(zr, to_z(k).start if k == 0 else to_dg.start)
+        if k == 0:
             when_in(far, to_far.start)
     place(REACH - to_core)
     pair_own.start()
@@ -412,8 +407,8 @@
     place(REACH)
     pair_x.wait_recv()
     sumbuf[1] = gwin[slot_x] + fromp[1]
-    to_x(2).start()
-    for k in range(2):
+    to_x(1).start()
+    for k in range(1):
 
         def join(k=k):
             got(landed.at[0, chunks[k]], g_recv.at[3 + k])
@@ -429,12 +424,12 @@
         out[...] += landed[2]
 
     def join_dg():
-        got(landed.at[0, chunks[2]], g_recv.at[5])
-        out[chunks[2]] += landed[0, chunks[2]]
+        got(landed.at[0, chunks[1]], g_recv.at[4])
+        out[chunks[1]] += landed[0, chunks[1]]
 
     when_in(far, join_far)
     when_in(zr, join_dg)
-    for k in (2, 0, 1):
+    for k in (1, 0):
         got(landed.at[1, chunks[k]], g_recv.at[k])
 
     lane = lax.broadcasted_iota(jnp.int32, (1, 128), 1)

time: 35.7 us -> 35.2 us (0.986)
  Pallas kernels: 32.6 us -> 32.1 us
    pallas_call x1, Pallas kernels: 32.6 us -> 32.1 us  [on_device(): pl.pallas_call(functools.partial(kernel, tiles), out_shape=jax.ShapeDtype...]
where the time goes in v7:
time: 35.2 us; the launch traced here: 35 us
  Pallas kernels  32.1 us (91%)
  local copies, waits for them, and re-layouts  1.59 us (5%)
  between operations  1.3 us (4%)
    pallas_call x1, Pallas kernels, on_device(): pl.pallas_call(functools.partial(kernel, tiles), out_shape=jax.ShapeDtype...  32.1 us
    unnamed x1, local copies, waits for them, and re-layouts  1.59 us

profile of v7, /device:TPU:0, one launch (start us, length us, event | category | flops | bytes accessed | tf_op | source)
XLA Modules:
  0.0 35.0 jit_solution(12418589946515508256)
XLA Ops:
  1.3 32.1 %shard_map.73 = f32[5,2,16,256]{3,2,1,0:T(8,128)} custom-call(s32[1]{0:T(128)S(6)} %copy.10.offsets, s32[1,1]{1,0:T(1,128)S(6)} %copy.9.sources, f32[5,2,16,256]{3,2,1,0:T(8,128)} %params.1, f32[1,1,9,8,16,256]{5,4,3,2,1,0:T(8,128)} %adjoint.1, bf16[1,1,6,3,8,16,256]{6,5,4,3,2,1,0:T(8,128)(2,1)} %snapshots.1, f32[6,1,256]{2,1,0:T(1,128)} %bitcast.2, ...), custom_call_target="tpu_custom_call" | custom-call | tf_op jit(solution)/shard_map/pallas_call | solution.py:483
  33.4 1.6 %copy.11 = f32[5,2,16,256]{3,2,1,0:T(8,128)} copy(f32[5,2,16,256]{3,2,1,0:T(8,128)} %shard_map.73) | data formatting | bytes 327680
